TPU v7x, 768 devices: a whole 4x8x12 slice. The times are simulated.
768 devices in a mesh: gy: 96 (over z, y), gx: 8 (over x, core).
Axes of the slice: x: 4, y: 8, z: 12, core: 2. Of those that a mesh axis runs over, the one named last changes fastest.
Arguments:
- sea_level: float32 [11520, 2048], P('gy', 'gx'), may hold values from -4 to 4
- transport_x: float32 [11520, 2048], P('gy', 'gx'), may hold values from -5 to 5
- transport_y: float32 [11520, 2048], P('gy', 'gx'), may hold values from -5 to 5
- friction: float32 [11520, 2048], P('gy', 'gx'), may hold values from 0.05 to 0.5
- levels: int32 [11520, 2048], P('gy', 'gx'), may hold values from 15 to 60
- strip_map: int32 [11520], P('gy'), may hold values from 0 to 2303, as said below
- parent_strip: float32 [2, 4, 2, 2304], P(None, None, None, ('gy', 'gx')), may hold values from -5 to 5
- plat_tile: int32 [3072], replicated, may hold values from 0 to 767
- plat_row: int32 [3072], replicated, may hold values from 0 to 119
- plat_col: int32 [3072], replicated, may hold values from 0 to 255
- plat_drag: float32 [60, 3072], P(None, ('gy', 'gx')), may hold values from 0.05 to 0.5
- plat_shear: float32 [2, 60, 3072], P(None, None, ('gy', 'gx')), may hold values from -3 to 3
Outputs:
- sea_out: float32 [11520, 2048], P('gy', 'gx')
- flow_x: float32 [11520, 2048], P('gy', 'gx')
- flow_y: float32 [11520, 2048], P('gy', 'gx')
Inputs may be any that keep to these rules, and one draw needn't show every extreme that they name: For a child row in row block g (rows g * 120 to g * 120 + 119) strip_map lies within g * 24 - 1 to g * 24 + 24.
All inputs are finite; a program needn't handle non-finite values.
Results may differ from a plain program's by a relative error of at most 0.00002.
Values sent between devices are 32-bit elements; how exact they have to be, the bound alone decides.
No kernel may reach another device: no remote copies, remote signals or barrier semaphores. Data moves between devices by JAX's collectives and lax.ppermute only.
A program may use at most 32 MiB of HBM per device.

v0:
```python
import jax
import jax.numpy as jnp
from jax import lax
from jax.sharding import PartitionSpec as P

SUBSTEPS = 4
LEVELS = 60


C_MASS = 0.5
C_MOMENTUM = 0.8
FRIC_STEP = 0.5
LOAD_GAIN = 0.5
FLATHER = 0.7


def padded_2(block, sides, width):
    for axis, dim in sides:
        count = lax.axis_size(axis)
        forward = [(i, i + 1) for i in range(count - 1)]
        backward = [(target, source) for source, target in forward]
        low = lax.ppermute(
            lax.slice_in_dim(block, block.shape[dim] - width, None, axis=dim), axis, forward
        )
        high = lax.ppermute(lax.slice_in_dim(block, 0, width, axis=dim), axis, backward)
        block = jnp.concatenate([low, block, high], axis=dim)
    return block


def morison(ubar, vbar, wet_count, drag, shear):
    depth_index = jnp.arange(LEVELS, dtype=jnp.float32)[:, None]
    wet = depth_index < wet_count[None, :]
    ux = ubar[None, :] + shear[0]
    uy = vbar[None, :] + shear[1]
    speed = jnp.sqrt(ux * ux + uy * uy)
    load_x = jnp.sum(jnp.where(wet, drag * speed * ux, 0.0), axis=0) / LEVELS
    load_y = jnp.sum(jnp.where(wet, drag * speed * uy, 0.0), axis=0) / LEVELS
    return jnp.stack([load_x, load_y])


def on_device(
    sea_level,
    transport_x,
    transport_y,
    friction,
    levels,
    strip_map,
    parent_strip,
    plat_tile,
    plat_row,
    plat_col,
    plat_drag,
    plat_shear,
):
    rows, cols = sea_level.shape
    col_count = lax.axis_size("gx")
    row_count = lax.axis_size("gy")
    row_block = lax.axis_index("gy")
    col_block = lax.axis_index("gx")
    tile = row_block * col_count + col_block
    depth = levels.astype(jnp.float32) / LEVELS
    owned = plat_tile == tile
    flat_cell = jnp.where(owned, plat_row * cols + plat_col, 0)
    pick_u = transport_x.reshape(-1)[flat_cell]
    pick_v = transport_y.reshape(-1)[flat_cell]
    pick_wet = levels.reshape(-1)[flat_cell].astype(jnp.float32)
    state = jnp.stack(
        [
            jnp.where(owned, pick_u, 0.0),
            jnp.where(owned, pick_v, 0.0),
            jnp.where(owned, pick_wet, 0.0),
        ]
    )
    total = lax.psum(state, ("gy", "gx"))
    count = plat_drag.shape[1]
    start = lax.axis_index(("gy", "gx")) * count
    mine = lax.dynamic_slice_in_dim(total, start, count, 1)
    held_depth = mine[2] / LEVELS
    loads_mine = morison(mine[0] / held_depth, mine[1] / held_depth, mine[2], plat_drag, plat_shear)
    loads = lax.all_gather(loads_mine, ("gy", "gx"), axis=1, tiled=True)
    load_x = jnp.where(owned, loads[0], 0.0)
    load_y = jnp.where(owned, loads[1], 0.0)
    force_x = jnp.zeros_like(sea_level).at[plat_row, plat_col].add(load_x)
    force_y = jnp.zeros_like(sea_level).at[plat_row, plat_col].add(load_y)
    block = lax.all_gather(parent_strip, "gx", axis=3, tiled=True)
    widened = padded_2(block, (("gy", 3),), 1)
    block_cells = block.shape[3]
    local_index = strip_map - row_block * block_cells + 1
    bound = jnp.take(widened, local_index, axis=3)
    west_tile = col_block == 0
    east_tile = col_block == col_count - 1
    global_rows = row_block * rows + jnp.arange(rows + 2, dtype=jnp.int32) - 1
    global_cols = col_block * cols + jnp.arange(cols + 2, dtype=jnp.int32) - 1
    row_inside = (global_rows >= 0) & (global_rows < row_count * rows)
    col_inside = (global_cols >= 0) & (global_cols < col_count * cols)
    inside = row_inside[:, None] & col_inside[None, :]
    fields = jnp.stack([sea_level, transport_x, transport_y])
    for step in range(SUBSTEPS):
        padded = padded_2(fields, (("gy", 1), ("gx", 2)), 2)
        pad_e = padded[0]
        pad_u = padded[1]
        pad_v = padded[2]
        flow_u = fields[1]
        flow_v = fields[2]
        mid = pad_e[1:-1, 1:-1] - C_MASS * (
            pad_u[1:-1, 2:] - pad_u[1:-1, :-2] + (pad_v[2:, 1:-1] - pad_v[:-2, 1:-1])
        )
        mid = jnp.where(inside, mid, 0.0)
        denom = 1.0 + FRIC_STEP * friction * jnp.sqrt(flow_u * flow_u + flow_v * flow_v) / (
            depth * depth
        )
        new_u = (
            flow_u - C_MOMENTUM * depth * (mid[1:-1, 2:] - mid[1:-1, :-2]) - LOAD_GAIN * force_x
        ) / denom
        new_v = (
            flow_v - C_MOMENTUM * depth * (mid[2:, 1:-1] - mid[:-2, 1:-1]) - LOAD_GAIN * force_y
        ) / denom
        center = mid[1:-1, 1:-1]
        west = bound[0, step, 1] - FLATHER * jnp.sqrt(depth[:, 0]) * (
            center[:, 0] - bound[0, step, 0]
        )
        east = bound[1, step, 1] + FLATHER * jnp.sqrt(depth[:, -1]) * (
            center[:, -1] - bound[1, step, 0]
        )
        new_u = new_u.at[:, 0].set(jnp.where(west_tile, west, new_u[:, 0]))
        new_u = new_u.at[:, -1].set(jnp.where(east_tile, east, new_u[:, -1]))
        fields = jnp.stack([center, new_u, new_v])
    return (fields[0], fields[1], fields[2])


def solution(mesh):
    return jax.shard_map(
        on_device,
        mesh=mesh,
        in_specs=(
            P("gy", "gx"),
            P("gy", "gx"),
            P("gy", "gx"),
            P("gy", "gx"),
            P("gy", "gx"),
            P("gy"),
            P(None, None, None, ("gy", "gx")),
            P(),
            P(),
            P(),
            P(None, ("gy", "gx")),
            P(None, None, ("gy", "gx")),
        ),
        out_specs=(P("gy", "gx"), P("gy", "gx"), P("gy", "gx")),
        check_vma=False,
    )
```

profile of v0, /device:TPU:1, one launch (start us, length us, event | category | flops | bytes accessed | tf_op | source)
XLA Modules:
  0.0 409.6 jit_solution(989878463157018375)
XLA Ops:
  0.7 0.8 pad_maximum_fusion.21
  1.5 4.0 collective-permute-start
  5.5 1.3 collective-permute-start.1
  6.8 20.4 %all_gather.7 = f32[2,4,2,24]{1,2,0,3:T(2,128)S(1)} all-gather(f32[2,4,2,3]{1,2,0,3:T(2,128)S(1)} %copy.106), channel_id=1, replica_groups=mesh['gy'=96,'gx'=8] {'gx'}, dimensions={3}, use_global_device_ids=true | all-gather | bytes 1728 | tf_op jit(solution)/shard_map/all_gather | solution.py:85
  27.2 4.3 %collective-permute-start.4 = (f32[2,4,2,1]{1,2,3,0:T(2,128)S(1)}, f32[2,4,2,1]{1,2,3,0:T(2,128)S(1)}, u32[]{:S(2)}, u32[]{:S(2)}) collective-permute-start(f32[2,4,2,1]{1,2,3,0:T(2,128)S(1)} %get-tuple-element.165), channel_id=1, source_target_pairs={{0,8},{8,16},{16,24},{24,32},{32,40},{40,48},{48,56},{56,64},{64,7... | collective-permute-start | bytes 200 | tf_op jit(solution)/shard_map/ppermute | solution.py:22
  31.5 1.3 collective-permute-start.5
  32.8 0.6 compare_reduce_fusion
  33.5 0.8 copy-done.1
  34.4 0.6 copy-done.6
  35.1 17.4 %gather_fusion = f32[3072]{0:T(1024)S(1)} fusion(f32[30720]{0:T(1024)S(1)} %bitcast.100, s32[3072]{0:T(1024)S(1)} %get-tuple-element.106), kind=kCustom, calls=%fused_computation | custom fusion | bytes 36864 | tf_op jit(solution)/shard_map/gather | solution.py:64
  52.5 17.4 %gather_fusion.1 = f32[3072]{0:T(1024)S(1)} fusion(f32[30720]{0:T(1024)S(1)} %bitcast.99, s32[3072]{0:T(1024)S(1)} %get-tuple-element.106), kind=kCustom, calls=%fused_computation.1 | custom fusion | bytes 36864 | tf_op jit(solution)/shard_map/gather | solution.py:65
  70.0 17.4 %gather_fusion.2 = s32[3072]{0:T(1024)S(1)} fusion(s32[30720]{0:T(1024)S(1)} %bitcast.101, s32[3072]{0:T(1024)S(1)} %get-tuple-element.106), kind=kCustom, calls=%fused_computation.2 | custom fusion | bytes 36864 | tf_op jit(solution)/shard_map/gather | solution.py:66
  87.5 115.0 %psum.7 = f32[3,3072]{1,0:T(4,128)S(1)} all-reduce(f32[3,3072]{1,0:T(4,128)S(1)} %pad_maximum_fusion.9), channel_id=1, replica_groups=mesh['gy'=96,'gx'=8] {'gy','gx'}, use_global_device_ids=true, to_apply=%region_0.1 | all-reduce | flops 9216 | bytes 73728 | tf_op jit(solution)/shard_map/psum | solution.py:74
  202.6 0.7 copy-done.10
  203.5 93.6 %all-gather = f32[768,4,2]{1,2,0:T(2,128)S(1)} all-gather(f32[1,4,2]{1,2,0:T(2,128)S(1)} %maximum_bitcast_fusion), channel_id=1, replica_groups=mesh['gy'=96,'gx'=8] {'gy','gx'}, dimensions={0}, use_global_device_ids=true | all-gather | bytes 24608 | tf_op jit(solution)/shard_map/all_gather | solution.py:80
  297.1 0.5 reshape.313
  297.6 0.6 copy-done.13
  298.4 0.6 copy-done.12
  299.1 16.6 %scatter_custom_fusion = f32[30720]{0:T(1024)S(1)} fusion(s32[3072]{0:T(1024)S(1)} %broadcast_select_fusion, f32[3072]{0:T(1024)S(1)} %get-tuple-element.171, f32[]{:T(128)} %constant.236.clone.1), kind=kCustom, calls=%fused_computation.140 | custom fusion | flops 3072 | bytes 122884
  315.7 16.6 %scatter_custom_fusion.1 = f32[30720]{0:T(1024)S(1)} fusion(s32[3072]{0:T(1024)S(1)} %broadcast_select_fusion, f32[3072]{0:T(1024)S(1)} %get-tuple-element.172, f32[]{:T(128)} %constant.236.clone.1), kind=kCustom, calls=%fused_computation.138 | custom fusion | flops 3072 | bytes 122884
  332.5 0.6 copy-done.14
  333.2 0.9 gather_fusion.3
  334.3 0.7 copy-done.4
  335.2 2.5 collective-permute-start.2
  337.7 1.9 collective-permute-start.3
  339.6 1.7 fusion.76
  341.3 3.4 collective-permute-done.3
  345.1 0.3 and_select_fusion.3
  345.4 0.6 copy-done.3
  346.2 0.7 select_select_fusion.3
  347.3 0.4 scatter.29
  347.7 2.2 collective-permute-start.6
  349.8 1.3 collective-permute-start.7
  351.1 3.1 collective-permute-done.7
  354.4 3.2 collective-permute-start.8
  357.5 2.1 collective-permute-start.9
  359.7 0.5 collective-permute-done.8
  360.1 4.4 %collective-permute-done.9 = f32[3,124,2]{2,1,0:T(8,128)S(1)} collective-permute-done((f32[3,124,2]{2,1,0:T(8,128)S(1)}, f32[3,124,2]{2,1,0:T(8,128)S(1)}, u32[]{:S(2)}, u32[]{:S(2)}) %collective-permute-start.9) | collective-permute-done | bytes 3008 | tf_op jit(solution)/shard_map/ppermute | solution.py:25
  364.9 0.3 and_select_fusion.2
  365.4 0.7 select_select_fusion.2
  366.5 0.4 scatter.31
  366.9 3.1 collective-permute-start.10
  370.0 1.3 collective-permute-start.11
  371.3 3.1 collective-permute-done.11
  374.6 3.1 collective-permute-start.12
  377.7 1.9 collective-permute-start.13
  379.7 0.7 collective-permute-done.12
  380.3 4.4 %collective-permute-done.13 = f32[3,124,2]{2,1,0:T(8,128)S(1)} collective-permute-done((f32[3,124,2]{2,1,0:T(8,128)S(1)}, f32[3,124,2]{2,1,0:T(8,128)S(1)}, u32[]{:S(2)}, u32[]{:S(2)}) %collective-permute-start.13) | collective-permute-done | bytes 3008 | tf_op jit(solution)/shard_map/ppermute | solution.py:25
  384.7 0.3 pad_maximum_fusion.2
  385.1 0.3 and_select_fusion.1
  385.6 0.7 select_select_fusion.1
  386.7 0.4 scatter.35
  387.1 4.1 collective-permute-start.14
  391.2 1.3 collective-permute-start.15
  392.5 3.3 collective-permute-done.15
  396.0 2.9 collective-permute-start.16
  398.9 1.9 collective-permute-start.17
  400.8 0.7 collective-permute-done.16
  401.5 4.4 %collective-permute-done.17 = f32[3,124,2]{2,1,0:T(8,128)S(1)} collective-permute-done((f32[3,124,2]{2,1,0:T(8,128)S(1)}, f32[3,124,2]{2,1,0:T(8,128)S(1)}, u32[]{:S(2)}, u32[]{:S(2)}) %collective-permute-start.17) | collective-permute-done | bytes 3008 | tf_op jit(solution)/shard_map/ppermute | solution.py:25
  406.2 0.3 and_select_fusion
  406.5 0.9 fusion.15
  407.4 0.7 select_select_fusion
  408.6 0.4 scatter.39
  408.9 0.6 copy-done.5
  (87 shorter events, 5.1 us)
Async XLA Ops:
  0.6 6.2 %copy-start.9 = (f32[2,4,2,3]{1,2,3,0:T(2,128)S(1)}, f32[2,4,2,3]{1,2,3,0:T(2,128)}, u32[]{:S(2)}) copy-start(f32[2,4,2,3]{1,2,3,0:T(2,128)} %param.34) | copy-start | bytes 580
  0.6 32.8 %copy-start = (f32[120,256]{1,0:T(8,128)S(1)}, f32[120,256]{1,0:T(8,128)}, u32[]{:S(2)}) copy-start(f32[120,256]{1,0:T(8,128)} %param.29) | copy-start | bytes 368644
  1.5 332.8 %collective-permute-start = (f32[3,2,256]{2,1,0:T(2,128)S(1)}, f32[3,2,256]{2,1,0:T(2,128)S(1)}, u32[]{:S(2)}, u32[]{:S(2)}) collective-permute-start(f32[3,2,256]{2,1,0:T(2,128)S(1)} %get-tuple-element.142), channel_id=1, source_target_pairs={{0,8},{8,16},{16,24},{24,32},{32,40},{40,48},{48,56},{56,64},{64,7... | collective-permute-start | bytes 18440 | tf_op jit(solution)/shard_map/ppermute | solution.py:22
  5.5 328.8 %collective-permute-start.1 = (f32[3,2,256]{2,1,0:T(2,128)S(1)}, f32[3,2,256]{2,1,0:T(2,128)S(1)}, u32[]{:S(2)}, u32[]{:S(2)}) collective-permute-start(f32[3,2,256]{2,1,0:T(2,128)S(1)} %get-tuple-element.143), channel_id=1, source_target_pairs={{8,0},{16,8},{24,16},{32,24},{40,32},{48,40},{56,48},{64,56},{72,6... | collective-permute-start | bytes 18440 | tf_op jit(solution)/shard_map/ppermute | solution.py:25
  27.2 305.9 %collective-permute-start.4 = (f32[2,4,2,1]{1,2,3,0:T(2,128)S(1)}, f32[2,4,2,1]{1,2,3,0:T(2,128)S(1)}, u32[]{:S(2)}, u32[]{:S(2)}) collective-permute-start(f32[2,4,2,1]{1,2,3,0:T(2,128)S(1)} %get-tuple-element.165), channel_id=1, source_target_pairs={{0,8},{8,16},{16,24},{24,32},{32,40},{40,48},{48,56},{56,64},{64,7... | collective-permute-start | bytes 200 | tf_op jit(solution)/shard_map/ppermute | solution.py:22
  31.5 301.7 %collective-permute-start.5 = (f32[2,4,2,1]{1,2,3,0:T(2,128)S(1)}, f32[2,4,2,1]{1,2,3,0:T(2,128)S(1)}, u32[]{:S(2)}, u32[]{:S(2)}) collective-permute-start(f32[2,4,2,1]{1,2,3,0:T(2,128)S(1)} %get-tuple-element.166), channel_id=1, source_target_pairs={{8,0},{16,8},{24,16},{32,24},{40,32},{48,40},{56,48},{64,56},{72,6... | collective-permute-start | bytes 200 | tf_op jit(solution)/shard_map/ppermute | solution.py:25
  33.4 0.9 copy-start.1
  34.3 0.7 copy-start.6
  34.3 0.7 copy-start.7
  34.3 0.7 copy-start.8
  52.5 17.4 %copy-start.2 = (s32[120,256]{1,0:T(8,128)S(1)}, s32[120,256]{1,0:T(8,128)}, u32[]{:S(2)}) copy-start(s32[120,256]{1,0:T(8,128)} %param.32) | copy-start | bytes 368644
  202.5 0.7 copy-start.10
  202.6 0.7 copy-start.11
  297.6 0.7 copy-start.13
  298.3 0.7 copy-start.12
  332.5 0.7 copy-start.14
  334.1 0.9 copy-start.4
  335.2 6.1 %collective-permute-start.2 = (f32[3,124,2]{2,1,0:T(8,128)S(1)}, f32[3,124,2]{2,1,0:T(8,128)S(1)}, u32[]{:S(2)}, u32[]{:S(2)}) collective-permute-start(f32[3,124,2]{2,1,0:T(8,128)S(1)} %get-tuple-element.134), channel_id=1, source_target_pairs={{0,1},{1,2},{2,3},{3,4},{4,5},{5,6},{6,7},{8,9},{9,10},{10,11},{11... | collective-permute-start | bytes 8936 | tf_op jit(solution)/shard_map/ppermute | solution.py:22
  337.7 7.0 %collective-permute-start.3 = (f32[3,124,2]{2,1,0:T(8,128)S(1)}, f32[3,124,2]{2,1,0:T(8,128)S(1)}, u32[]{:S(2)}, u32[]{:S(2)}) collective-permute-start(f32[3,124,2]{2,1,0:T(8,128)S(1)} %get-tuple-element.135), channel_id=1, source_target_pairs={{1,0},{2,1},{3,2},{4,3},{5,4},{6,5},{7,6},{9,8},{10,9},{11,10},{12... | collective-permute-start | bytes 8936 | tf_op jit(solution)/shard_map/ppermute | solution.py:25
  345.0 0.9 copy-start.3
  347.7 3.5 collective-permute-start.6
  349.8 4.4 %collective-permute-start.7 = (f32[3,2,256]{2,1,0:T(2,128)S(1)}, f32[3,2,256]{2,1,0:T(2,128)S(1)}, u32[]{:S(2)}, u32[]{:S(2)}) collective-permute-start(f32[3,2,256]{2,1,0:T(2,128)S(1)} %get-tuple-element.141), channel_id=1, source_target_pairs={{8,0},{16,8},{24,16},{32,24},{40,32},{48,40},{56,48},{64,56},{72,6... | collective-permute-start | bytes 18440 | tf_op jit(solution)/shard_map/ppermute | solution.py:25
  354.4 5.8 %collective-permute-start.8 = (f32[3,124,2]{2,1,0:T(8,128)S(1)}, f32[3,124,2]{2,1,0:T(8,128)S(1)}, u32[]{:S(2)}, u32[]{:S(2)}) collective-permute-start(f32[3,124,2]{2,1,0:T(8,128)S(1)} %get-tuple-element.132), channel_id=1, source_target_pairs={{0,1},{1,2},{2,3},{3,4},{4,5},{5,6},{6,7},{8,9},{9,10},{10,11},{11... | collective-permute-start | bytes 8936 | tf_op jit(solution)/shard_map/ppermute | solution.py:22
  357.5 7.0 %collective-permute-start.9 = (f32[3,124,2]{2,1,0:T(8,128)S(1)}, f32[3,124,2]{2,1,0:T(8,128)S(1)}, u32[]{:S(2)}, u32[]{:S(2)}) collective-permute-start(f32[3,124,2]{2,1,0:T(8,128)S(1)} %get-tuple-element.133), channel_id=1, source_target_pairs={{1,0},{2,1},{3,2},{4,3},{5,4},{6,5},{7,6},{9,8},{10,9},{11,10},{12... | collective-permute-start | bytes 8936 | tf_op jit(solution)/shard_map/ppermute | solution.py:25
  366.9 4.4 %collective-permute-start.10 = (f32[3,2,256]{2,1,0:T(2,128)S(1)}, f32[3,2,256]{2,1,0:T(2,128)S(1)}, u32[]{:S(2)}, u32[]{:S(2)}) collective-permute-start(f32[3,2,256]{2,1,0:T(2,128)S(1)} %get-tuple-element.138), channel_id=1, source_target_pairs={{0,8},{8,16},{16,24},{24,32},{32,40},{40,48},{48,56},{56,64},{64,7... | collective-permute-start | bytes 18440 | tf_op jit(solution)/shard_map/ppermute | solution.py:22
  370.0 4.4 %collective-permute-start.11 = (f32[3,2,256]{2,1,0:T(2,128)S(1)}, f32[3,2,256]{2,1,0:T(2,128)S(1)}, u32[]{:S(2)}, u32[]{:S(2)}) collective-permute-start(f32[3,2,256]{2,1,0:T(2,128)S(1)} %get-tuple-element.139), channel_id=1, source_target_pairs={{8,0},{16,8},{24,16},{32,24},{40,32},{48,40},{56,48},{64,56},{72,6... | collective-permute-start | bytes 18440 | tf_op jit(solution)/shard_map/ppermute | solution.py:25
  374.6 5.7 %collective-permute-start.12 = (f32[3,124,2]{2,1,0:T(8,128)S(1)}, f32[3,124,2]{2,1,0:T(8,128)S(1)}, u32[]{:S(2)}, u32[]{:S(2)}) collective-permute-start(f32[3,124,2]{2,1,0:T(8,128)S(1)} %get-tuple-element.130), channel_id=1, source_target_pairs={{0,1},{1,2},{2,3},{3,4},{4,5},{5,6},{6,7},{8,9},{9,10},{10,11},{11... | collective-permute-start | bytes 8936 | tf_op jit(solution)/shard_map/ppermute | solution.py:22
  377.7 7.0 %collective-permute-start.13 = (f32[3,124,2]{2,1,0:T(8,128)S(1)}, f32[3,124,2]{2,1,0:T(8,128)S(1)}, u32[]{:S(2)}, u32[]{:S(2)}) collective-permute-start(f32[3,124,2]{2,1,0:T(8,128)S(1)} %get-tuple-element.131), channel_id=1, source_target_pairs={{1,0},{2,1},{3,2},{4,3},{5,4},{6,5},{7,6},{9,8},{10,9},{11,10},{12... | collective-permute-start | bytes 8936 | tf_op jit(solution)/shard_map/ppermute | solution.py:25
  387.1 5.4 %collective-permute-start.14 = (f32[3,2,256]{2,1,0:T(2,128)S(1)}, f32[3,2,256]{2,1,0:T(2,128)S(1)}, u32[]{:S(2)}, u32[]{:S(2)}) collective-permute-start(f32[3,2,256]{2,1,0:T(2,128)S(1)} %get-tuple-element.136), channel_id=1, source_target_pairs={{0,8},{8,16},{16,24},{24,32},{32,40},{40,48},{48,56},{56,64},{64,7... | collective-permute-start | bytes 18440 | tf_op jit(solution)/shard_map/ppermute | solution.py:22
  391.2 4.7 %collective-permute-start.15 = (f32[3,2,256]{2,1,0:T(2,128)S(1)}, f32[3,2,256]{2,1,0:T(2,128)S(1)}, u32[]{:S(2)}, u32[]{:S(2)}) collective-permute-start(f32[3,2,256]{2,1,0:T(2,128)S(1)} %get-tuple-element.137), channel_id=1, source_target_pairs={{8,0},{16,8},{24,16},{32,24},{40,32},{48,40},{56,48},{64,56},{72,6... | collective-permute-start | bytes 18440 | tf_op jit(solution)/shard_map/ppermute | solution.py:25
  396.0 5.5 %collective-permute-start.16 = (f32[3,124,2]{2,1,0:T(8,128)S(1)}, f32[3,124,2]{2,1,0:T(8,128)S(1)}, u32[]{:S(2)}, u32[]{:S(2)}) collective-permute-start(f32[3,124,2]{2,1,0:T(8,128)S(1)} %get-tuple-element.128), channel_id=1, source_target_pairs={{0,1},{1,2},{2,3},{3,4},{4,5},{5,6},{6,7},{8,9},{9,10},{10,11},{11... | collective-permute-start | bytes 8936 | tf_op jit(solution)/shard_map/ppermute | solution.py:22
  398.9 7.0 %collective-permute-start.17 = (f32[3,124,2]{2,1,0:T(8,128)S(1)}, f32[3,124,2]{2,1,0:T(8,128)S(1)}, u32[]{:S(2)}, u32[]{:S(2)}) collective-permute-start(f32[3,124,2]{2,1,0:T(8,128)S(1)} %get-tuple-element.129), channel_id=1, source_target_pairs={{1,0},{2,1},{3,2},{4,3},{5,4},{6,5},{7,6},{9,8},{10,9},{11,10},{12... | collective-permute-start | bytes 8936 | tf_op jit(solution)/shard_map/ppermute | solution.py:25
  408.9 0.7 copy-start.5
where the time goes:
time: 411 us; the launch traced here: 410 us
  blocking collectives  229 us (56%)
  local copies, waits for them, and re-layouts  64.7 us (16%)
  starting transfers between devices  43.6 us (11%)
  other arithmetic  42.9 us (10%)
  waiting for transfers between devices  27.9 us (7%)
    psum x1, blocking collectives, on_device(): total = lax.psum(state, ('gy', 'gx'))  115 us
    all_gather x1, blocking collectives, on_device(): loads = lax.all_gather(loads_mine, ('gy', 'gx'), axis=1, tiled=True)  93.6 us
    unnamed x6, other arithmetic  33.4 us
    ppermute x9, starting transfers between devices, padded_2(): lax.ppermute(lax.slice_in_dim(block, block.shape[dim] - width, None, axis...  29.3 us
    ppermute x9, waiting for transfers between devices, padded_2(): lax.ppermute(lax.slice_in_dim(block, 0, width, axis=dim), axis, backward)  26.1 us
    all_gather x1, blocking collectives, on_device(): block = lax.all_gather(parent_strip, 'gx', axis=3, tiled=True)  20.4 us
    gather x1, local copies, waits for them, and re-layouts, on_device(): pick_u = transport_x.reshape(-1)[flat_cell]  17.4 us
    gather x1, local copies, waits for them, and re-layouts, on_device(): pick_v = transport_y.reshape(-1)[flat_cell]  17.4 us
  transfers between devices with their start and end apart: 18, of which 10 were waited for; matrix products, arithmetic and copies ran while one was open for 22% of the time, Pallas kernels for 0%

commit v1 on v0

v1 whole, which is shorter than its diff:
```python
import functools

import jax
import jax.numpy as jnp
from jax import lax
from jax.experimental import pallas as pl
from jax.experimental.pallas import tpu as pltpu
from jax.sharding import PartitionSpec as P

SUBSTEPS = 4
LEVELS = 60

C_MASS = 0.5
C_MOMENTUM = 0.8
FRIC_STEP = 0.5
LOAD_GAIN = 0.5
FLATHER = 0.7

ROWS = 120
COLS = 256
N_GX = 8
N_GY = 96
HELD = 4
PLAT = N_GY * N_GX * HELD
COL_PLAT = N_GY * HELD

HALO = 2 * SUBSTEPS
EXT = ROWS + 2 * HALO
WIDE = COLS + 128
GROUP = 48
FIELDS = 5
SPAN = FIELDS * HALO
CELL_ROW = GROUP
STRIP_ROW = GROUP + 9
SLOT_ROWS = 64
CHUNK = 512


def iota(shape, dim):
    return lax.broadcasted_iota(jnp.int32, shape, dim)


def three_parts(x):
    high = x.astype(jnp.bfloat16).astype(jnp.float32)
    rest = x - high
    middle = rest.astype(jnp.bfloat16).astype(jnp.float32)
    return [high, middle, rest - middle]


def decode(code):
    col = jnp.bitwise_and(code, COLS - 1)
    row = jnp.bitwise_and(jnp.right_shift(code, 8), 127)
    tile_x = jnp.bitwise_and(jnp.right_shift(code, 15), N_GX - 1)
    tile_y = jnp.right_shift(code, 18)
    return tile_y, tile_x, row, col


def column_of(row_vector):
    return jnp.transpose(jnp.broadcast_to(row_vector, (128, 128)))


def row_halo_kernel(eta, flow_u, flow_v, friction, levels, smap, top, bottom):
    last = ROWS - HALO
    for f, ref in enumerate((eta, flow_u, flow_v, friction, levels)):
        top[f * HALO : (f + 1) * HALO, :] = ref[:HALO, :].astype(jnp.float32)
        bottom[f * HALO : (f + 1) * HALO, :] = ref[last:, :].astype(jnp.float32)
    column = column_of(smap[...].astype(jnp.float32))
    for half in (slice(0, 128), slice(128, 256)):
        top[FIELDS * HALO :, half] = column[:HALO]
        bottom[FIELDS * HALO :, half] = column[last:ROWS]


def extended(f, ref, up, down):
    part = slice(f * HALO, (f + 1) * HALO)
    return jnp.concatenate([up[part, :], ref[...].astype(jnp.float32), down[part, :]], axis=0)


def cell_kernel(pos, eta, flow_u, flow_v, friction, levels, up, down, code, raw, slots):
    gy = pos[0]
    gx = pos[1]
    wide = [
        extended(f, ref, up, down)
        for f, ref in enumerate((eta, flow_u, flow_v, friction, levels))
    ]
    stack = three_parts(wide[1]) + three_parts(wide[2]) + [wide[4]]
    stack.append(jnp.zeros((HALO, COLS), jnp.float32))
    table = jnp.concatenate(stack, axis=0).astype(jnp.bfloat16)
    for start in range(0, PLAT, CHUNK):
        tile_y, tile_x, row, col = decode(code[:, start : start + CHUNK])
        place = (tile_y - gy) * ROWS + row + HALO
        near = (tile_x == gx) & (place >= 0) & (place < EXT)
        hot = iota((COLS, CHUNK), 0) == jnp.where(near, col, -1)
        found = jnp.dot(
            table, hot.astype(jnp.bfloat16), preferred_element_type=jnp.float32
        )
        mine = iota((EXT, CHUNK), 0) == place
        parts = [found[n * EXT : (n + 1) * EXT] for n in range(7)]
        values = [
            parts[0] + parts[1] + parts[2],
            parts[3] + parts[4] + parts[5],
            parts[6],
        ]
        for f, value in enumerate(values):
            line = jnp.sum(jnp.where(mine, value, 0.0), axis=0, keepdims=True)
            for b in range(CHUNK // 128):
                block = start // 128 + b
                r = CELL_ROW + 3 * f + block % 3
                slots[block // 3, r : r + 1, :] = line[:, b * 128 : (b + 1) * 128]
    lane = iota((GROUP, 128), 1)
    west = jnp.zeros((GROUP, 128), jnp.float32)
    east = jnp.zeros((GROUP, 128), jnp.float32)
    for f in range(FIELDS):
        tall = jnp.concatenate(
            [wide[f], jnp.zeros((3 * GROUP - EXT, COLS), jnp.float32)], axis=0
        )
        for g in range(3):
            at = g * SPAN + f * HALO
            rows = slice(g * GROUP, (g + 1) * GROUP)
            mask = (lane >= at) & (lane < at + HALO)
            moved = pltpu.roll(tall[rows, :128], at, 1)
            west = jnp.where(mask, moved, west)
            moved = pltpu.roll(tall[rows, 128:], (at + HALO) % 128, 1)
            east = jnp.where(mask, moved, east)
    for j in range(N_GX):
        slots[j, :GROUP, :] = jnp.where(j > gx, east, west)
    lane = iota((1, 128), 1)
    for b in range(5):
        block = raw[jnp.clip(gy - 2 + b, 0, N_GY - 1)]
        strip = jnp.zeros((1, 128), jnp.float32)
        for t in range(6):
            moved = pltpu.roll(block[t : t + 1, :], (4 * t - 60) % 128, 1)
            strip = jnp.where(jnp.right_shift(jnp.bitwise_and(lane, 63), 2) == t, moved, strip)
        for j in range(N_GX):
            slots[j, STRIP_ROW + b : STRIP_ROW + b + 1, :] = strip
    for j in range(N_GX):
        slots[j, STRIP_ROW + 5 :, :] = jnp.zeros((SLOT_ROWS - STRIP_ROW - 5, 128), jnp.float32)


def load_kernel(raw, cells, slots):
    total = cells[0, CELL_ROW : CELL_ROW + 9, :]
    for j in range(1, N_GX):
        total = total + cells[j, CELL_ROW : CELL_ROW + 9, :]
    lines = []
    for f in range(3):
        line = jnp.concatenate([total[3 * f + q : 3 * f + q + 1, :] for q in range(3)], axis=1)
        for i in range(HELD):
            part = line[:, i * N_GY : (i + 1) * N_GY]
            lines.append(
                jnp.concatenate([part, jnp.zeros((1, 128 - N_GY), jnp.float32)], axis=1)
            )
    lines.append(jnp.zeros((128 - len(lines), 128), jnp.float32))
    columns = jnp.transpose(jnp.concatenate(lines, axis=0))[:N_GY]
    lane = iota((N_GY, 128), 1)
    low = lane < 64
    level = jnp.bitwise_and(lane, 63).astype(jnp.float32)
    result = jnp.zeros((N_GY, 128), jnp.float32)
    for q in range(2):
        u, v, wet = [
            jnp.where(
                low,
                columns[:, f * HELD + 2 * q : f * HELD + 2 * q + 1],
                columns[:, f * HELD + 2 * q + 1 : f * HELD + 2 * q + 2],
            )
            for f in range(3)
        ]
        depth = jnp.maximum(wet, 1.0) / LEVELS
        ux = u / depth + raw[:, 2 + q, :]
        uy = v / depth + raw[:, 4 + q, :]
        drag = jnp.where(level < wet, raw[:, q, :] * jnp.sqrt(ux * ux + uy * uy), 0.0)
        for c, flow in enumerate((ux, uy)):
            product = drag * flow
            for h in range(2):
                share = jnp.where(low, product, 0.0) if h == 0 else jnp.where(low, 0.0, product)
                load = jnp.sum(share, axis=1, keepdims=True) / LEVELS
                result = jnp.where(lane == c * HELD + 2 * q + h, load, result)
    result = jnp.concatenate([result, jnp.zeros((128 - N_GY, 128), jnp.float32)], axis=0)
    rows = jnp.transpose(result)
    out = []
    for c in range(2):
        line = jnp.concatenate(
            [rows[c * HELD + i : c * HELD + i + 1, :N_GY] for i in range(HELD)], axis=1
        )
        out += [line[:, q * 128 : (q + 1) * 128] for q in range(3)]
    out.append(jnp.zeros((2, 128), jnp.float32))
    block = jnp.concatenate(out, axis=0)
    for j in range(N_GX):
        slots[j] = block


def step_kernel(
    pos, eta, flow_u, flow_v, friction, levels, smap, up, down, code, cells, loads,
    out_eta, out_u, out_v, force,
):
    gy = pos[0]
    gx = pos[1]
    for start in range(0, PLAT, CHUNK):
        tile_y, tile_x, row, col = decode(code[:, start : start + CHUNK])
        place = (tile_y - gy) * ROWS + row + HALO
        across = (tile_x - gx) * COLS + col
        near = (across >= -HALO) & (across < COLS + HALO)
        across = jnp.where(near, jnp.where(across < 0, across + WIDE, across), -1)
        mine = iota((EXT, CHUNK), 0) == place
        left = []
        for c in range(2):
            line = jnp.concatenate(
                [
                    loads[b // 3, 3 * c + b % 3 : 3 * c + b % 3 + 1, :]
                    for b in range(start // 128, (start + CHUNK) // 128)
                ],
                axis=1,
            )
            left += [jnp.where(mine, part, 0.0) for part in three_parts(line)]
        left = jnp.concatenate(left, axis=0).astype(jnp.bfloat16)
        right = (iota((WIDE, CHUNK), 0) == across).astype(jnp.bfloat16)
        product = lax.dot_general(
            left, right, (((1,), (1,)), ((), ())), preferred_element_type=jnp.float32
        )
        if start == 0:
            force[...] = product
        else:
            force[...] += product
    part = [force[n * EXT : (n + 1) * EXT, :] for n in range(6)]
    force_x = LOAD_GAIN * (part[0] + part[1] + part[2])
    force_y = LOAD_GAIN * (part[3] + part[4] + part[5])

    from_west = cells[jnp.maximum(gx - 1, 0), :GROUP, :]
    from_east = cells[jnp.minimum(gx + 1, N_GX - 1), :GROUP, :]
    lane = iota((GROUP, 128), 1)

    def widened(f, ref):
        side = []
        for g in range(3):
            at = g * SPAN + f * HALO
            east = pltpu.roll(from_east, (-at) % 128, 1)
            west = pltpu.roll(from_west, (120 - at) % 128, 1)
            side.append(jnp.where(lane < HALO, east, jnp.where(lane >= 120, west, 0.0)))
        side = jnp.concatenate(side, axis=0)[:EXT]
        return jnp.concatenate([extended(f, ref, up, down), side], axis=1)

    e, u, v, fric, lev = [
        widened(f, ref) for f, ref in enumerate((eta, flow_u, flow_v, friction, levels))
    ]
    row = iota((EXT, WIDE), 0)
    lane = iota((EXT, WIDE), 1)
    inside = ((row >= HALO) | (gy > 0)) & ((row < HALO + ROWS) | (gy < N_GY - 1))
    inside = inside & (
        (lane < COLS)
        | ((lane < COLS + HALO) & (gx < N_GX - 1))
        | ((lane >= WIDE - HALO) & (gx > 0))
    )
    e = jnp.where(inside, e, 0.0)
    u = jnp.where(inside, u, 0.0)
    v = jnp.where(inside, v, 0.0)
    depth = jnp.where(inside, lev / LEVELS, 1.0)
    rub = jnp.where(inside, FRIC_STEP * fric / (depth * depth), 1.0)
    push = C_MOMENTUM * depth

    ends = FIELDS * HALO
    ids = jnp.concatenate(
        [up[ends:, :128], column_of(smap[...].astype(jnp.float32))[:ROWS], down[ends:, :128]],
        axis=0,
    ).astype(jnp.int32)
    parents = jnp.concatenate(
        [cells[j, STRIP_ROW : STRIP_ROW + 5, :] for j in range(N_GX)]
        + [jnp.zeros((128 - 5 * N_GX, 128), jnp.float32)],
        axis=0,
    )
    source = iota((EXT, 128), 1)
    bound = jnp.zeros((EXT, 128), jnp.float32)
    slot_lane = jnp.right_shift(jnp.bitwise_and(iota((128, 128), 1), 63), 3)
    for j in range(3):
        column = jnp.zeros((EXT, 128), jnp.int32)
        for step in range(1, N_GX):
            column = column + (source >= 5 * step).astype(jnp.int32)
        block = gy - 2 + source - 5 * column
        held = (ids == (block * N_GX + column) * 3 + j) & (source < 5 * N_GX)
        part = jnp.where(slot_lane == j, parents, 0.0)
        bound = bound + sum(
            jnp.dot(
                held.astype(jnp.bfloat16),
                piece.astype(jnp.bfloat16),
                preferred_element_type=jnp.float32,
            )
            for piece in three_parts(part)
        )
    bound = bound + pltpu.roll(bound, 120, 1) + pltpu.roll(bound, 112, 1)

    side_lane = iota((EXT, 128), 1)
    at_west = (side_lane == 0) & (gx == 0)
    at_east = (side_lane == 127) & (gx == N_GX - 1)
    radiate_west = FLATHER * jnp.sqrt(depth[:, :128])
    radiate_east = FLATHER * jnp.sqrt(depth[:, 128:COLS])
    for step in range(SUBSTEPS):
        spread = pltpu.roll(u, WIDE - 1, 1) - pltpu.roll(u, 1, 1)
        spread = spread + (pltpu.roll(v, EXT - 1, 0) - pltpu.roll(v, 1, 0))
        mid = jnp.where(inside, e - C_MASS * spread, 0.0)
        denom = 1.0 + rub * jnp.sqrt(u * u + v * v)
        slope_x = pltpu.roll(mid, WIDE - 1, 1) - pltpu.roll(mid, 1, 1)
        slope_y = pltpu.roll(mid, EXT - 1, 0) - pltpu.roll(mid, 1, 0)
        scale = 1.0 / denom
        new_u = (u - push * slope_x - force_x) * scale
        new_v = (v - push * slope_y - force_y) * scale
        west = bound[:, 2 * step + 1 : 2 * step + 2] - radiate_west * (
            mid[:, :128] - bound[:, 2 * step : 2 * step + 1]
        )
        east = bound[:, 64 + 2 * step + 1 : 64 + 2 * step + 2] + radiate_east * (
            mid[:, 128:COLS] - bound[:, 64 + 2 * step : 64 + 2 * step + 1]
        )
        new_u = jnp.concatenate(
            [
                jnp.where(at_west, west, new_u[:, :128]),
                jnp.where(at_east, east, new_u[:, 128:COLS]),
                new_u[:, COLS:],
            ],
            axis=1,
        )
        e = mid
        u = jnp.where(inside, new_u, 0.0)
        v = jnp.where(inside, new_v, 0.0)
    out_eta[...] = e[HALO : HALO + ROWS, :COLS]
    out_u[...] = u[HALO : HALO + ROWS, :COLS]
    out_v[...] = v[HALO : HALO + ROWS, :COLS]


def call(kernel, out_shape, smem, count, name, scratch=()):
    vmem = pl.BlockSpec(memory_space=pltpu.VMEM)
    specs = [pl.BlockSpec(memory_space=pltpu.SMEM)] * smem + [vmem] * (count - smem)
    many = isinstance(out_shape, list)
    return pl.pallas_call(
        kernel,
        out_shape=out_shape,
        in_specs=specs,
        out_specs=[vmem] * len(out_shape) if many else vmem,
        scratch_shapes=list(scratch),
        compiler_params=pltpu.CompilerParams(vmem_limit_bytes=32 * 1024 * 1024),
        name=name,
    )


def f32(*shape):
    return jax.ShapeDtypeStruct(shape, jnp.float32)


def on_device(
    sea_level,
    transport_x,
    transport_y,
    friction,
    levels,
    strip_map,
    parent_strip,
    plat_tile,
    plat_row,
    plat_col,
    plat_drag,
    plat_shear,
):
    pos = jnp.stack([lax.axis_index("gy"), lax.axis_index("gx")]).astype(jnp.int32)
    fields = (sea_level, transport_x, transport_y, friction, levels)
    smap = jnp.pad(strip_map, (0, 128 - ROWS)).reshape(1, 128)
    top, bottom = call(row_halo_kernel, [f32(48, COLS), f32(48, COLS)], 0, 6, "row_halo")(
        *fields, smap
    )
    count = lax.axis_size("gy")
    upward = [(i, i + 1) for i in range(count - 1)]
    downward = [(target, source) for source, target in upward]
    up = lax.ppermute(bottom, "gy", upward)
    down = lax.ppermute(top, "gy", downward)

    held = jnp.concatenate([plat_drag[None], plat_shear], axis=0)
    held = held.transpose(0, 2, 1).reshape(6, 2, LEVELS)
    strip = parent_strip.reshape(2, 2, 4, 3).transpose(3, 1, 0, 2).reshape(6, 2, 4)
    held = jnp.concatenate([held, strip], axis=2).reshape(1, 6, 128)
    raw = lax.all_to_all(jnp.broadcast_to(held, (N_GY, 6, 128)), "gy", 0, 0, tiled=True)

    code = (plat_tile << 15) | (plat_row << 8) | plat_col
    code = code.reshape(N_GY, N_GX, HELD).transpose(1, 2, 0).reshape(1, PLAT)
    slots = call(cell_kernel, f32(N_GX, SLOT_ROWS, 128), 1, 10, "cells")(
        pos, *fields, up, down, code, raw
    )
    cells = lax.all_to_all(slots, "gx", 0, 0, tiled=True)
    slots = call(load_kernel, f32(N_GX, 8, 128), 0, 2, "loads")(raw, cells)
    loads = lax.all_to_all(slots, "gx", 0, 0, tiled=True)
    out = f32(ROWS, COLS)
    return tuple(
        call(
            step_kernel,
            [out, out, out],
            1,
            12,
            "steps",
            [pltpu.VMEM((6 * EXT, WIDE), jnp.float32)],
        )(pos, *fields, smap, up, down, code, cells, loads)
    )


def solution(mesh):
    return jax.shard_map(
        on_device,
        mesh=mesh,
        in_specs=(
            P("gy", "gx"),
            P("gy", "gx"),
            P("gy", "gx"),
            P("gy", "gx"),
            P("gy", "gx"),
            P("gy"),
            P(None, None, None, ("gy", "gx")),
            P(),
            P(),
            P(),
            P(None, ("gy", "gx")),
            P(None, None, ("gy", "gx")),
        ),
        out_specs=(P("gy", "gx"), P("gy", "gx"), P("gy", "gx")),
        check_vma=False,
    )
```

time: 411 us -> 78.9 us (0.19)
  blocking collectives: 229 us -> 22.1 us
  local copies, waits for them, and re-layouts: 64.7 us -> 3.09 us
  other arithmetic: 42.9 us -> 0.17 us
  starting transfers between devices: 43.6 us -> 26.8 us
  waiting for transfers between devices: 27.9 us -> 16.3 us
  Pallas kernels: 0 us -> 9.13 us
    psum x1 -> x0, blocking collectives: 115 us -> none  [on_device(): total = lax.psum(state, ('gy', 'gx'))]
    all_gather x2 -> x0, blocking collectives: 114 us -> none  [the longest x1 93.6 us: on_device(): loads = lax.all_gather(loads_mine, ('gy', 'gx'), axis=1, tiled=True)]
    gather x4 -> x0, local copies, waits for them, and re-layouts: 53.1 us -> none  [the longest x1 17.4 us: on_device(): pick_u = transport_x.reshape(-1)[flat_cell]]
    ppermute x18 -> x2, starting transfers between devices: 43.6 us -> 4.13 us  [the longest x1 2.83 us: on_device(): up = lax.ppermute(bottom, 'gy', upward)]
    unnamed x6 -> x0, other arithmetic: 33.4 us -> none
    ppermute x18 -> x2, waiting for transfers between devices: 27.9 us -> 3.56 us  [the longest x1 3.56 us: on_device(): down = lax.ppermute(top, 'gy', downward)]
    all_to_all x0 -> x1, starting transfers between devices: none -> 22.7 us  [on_device(): lax.all_to_all(jnp.broadcast_to(held, (N_GY, 6, 128)), 'gy', 0, 0, tiled=...]
    all_to_all x0 -> x2, blocking collectives: none -> 22.1 us  [the longest x1 14 us: on_device(): cells = lax.all_to_all(slots, 'gx', 0, 0, tiled=True)]
  transfers between devices with their start and end apart: 18 -> 3, of which waited for: 10 -> 2; matrix products, arithmetic and copies ran while one was open for 22% -> 1% of each run, Pallas kernels for 0% -> 0%
where the time goes in v1:
time: 78.9 us; the launch traced here: 78.5 us
  starting transfers between devices  26.8 us (34%)
  blocking collectives  22.1 us (28%)
  waiting for transfers between devices  16.3 us (21%)
  Pallas kernels  9.13 us (12%)
  local copies, waits for them, and re-layouts  3.09 us (4%)
  between operations  0.84 us (1%)
    all_to_all x1, starting transfers between devices, on_device(): lax.all_to_all(jnp.broadcast_to(held, (N_GY, 6, 128)), 'gy', 0, 0, tiled=...  22.7 us
    all_to_all x1, blocking collectives, on_device(): cells = lax.all_to_all(slots, 'gx', 0, 0, tiled=True)  14 us
    all_to_all x1, waiting for transfers between devices, on_device(): lax.all_to_all(jnp.broadcast_to(held, (N_GY, 6, 128)), 'gy', 0, 0, tiled=...  12.7 us
    all_to_all x1, blocking collectives, on_device(): loads = lax.all_to_all(slots, 'gx', 0, 0, tiled=True)  8.12 us
    pallas_call x1, Pallas kernels, on_device(): call(step_kernel, [out, out, out], 1, 12, 'steps', [pltpu.VMEM((6 * EXT,...  5.75 us
    ppermute x1, waiting for transfers between devices, on_device(): down = lax.ppermute(top, 'gy', downward)  3.56 us
    ppermute x1, starting transfers between devices, on_device(): up = lax.ppermute(bottom, 'gy', upward)  2.83 us
    pallas_call x1, Pallas kernels, on_device(): call(cell_kernel, f32(N_GX, SLOT_ROWS, 128), 1, 10, 'cells')  2.57 us
  transfers between devices with their start and end apart: 3, of which 2 were waited for; matrix products, arithmetic and copies ran while one was open for 1% of the time, Pallas kernels for 0%

profile of v1, /device:TPU:1, one launch (start us, length us, event | category | flops | bytes accessed | tf_op | source)
XLA Modules:
  0.0 78.5 jit_solution(7581187383070893398)
XLA Ops:
  0.6 0.8 %copy.18 = f32[2,4,2,3]{3,2,1,0:T(2,128)S(1)} copy(f32[2,4,2,3]{1,2,3,0:T(2,128)} %param.18) | data formatting | bytes 384 | tf_op args[6]
  1.4 0.0 copy-start.8
  1.4 0.0 copy-start.9
  1.4 0.1 copy.19
  1.5 0.6 copy-done.8
  2.1 0.0 copy-done.9
  2.1 0.1 pad_maximum_fusion.1
  2.2 0.1 broadcast_in_dim.11
  2.3 0.8 broadcast_in_dim.12
  3.1 0.0 copy-start.10
  3.1 0.0 copy-start
  3.1 0.0 copy-start.1
  3.1 0.0 copy-start.2
  3.1 0.0 copy-start.3
  3.1 0.0 copy-start.4
  3.1 22.7 %all-to-all-start = ((f32[96,6,128]{2,1,0:T(8,128)}), f32[96,6,128]{2,1,0:T(8,128)S(1)}, u32[]{:S(2)}, u32[]{:S(2)}) async-start(f32[96,6,128]{2,1,0:T(8,128)} %broadcast_in_dim.12), calls=%async_computation | async-start | bytes 786432 | tf_op jit(solution)/shard_map/all_to_all | solution.py:374
  25.8 0.0 copy-done.10
  25.8 0.0 copy-done
  25.8 0.0 copy-done.1
  25.8 0.0 copy-done.2
  25.9 0.0 copy-done.3
  25.9 0.0 copy-done.4
  25.9 0.0 copy-start.6
  25.9 0.0 copy-start.7
  25.9 0.1 row_halo.1
  26.0 0.0 copy-start.5
  26.0 2.8 %collective-permute-start = (f32[48,256]{1,0:T(8,128)S(1)}, f32[48,256]{1,0:T(8,128)S(1)}, u32[]{:S(2)}, u32[]{:S(2)}) collective-permute-start(f32[48,256]{1,0:T(8,128)S(1)} %get-tuple-element.5), channel_id=1, source_target_pairs={{0,8},{8,16},{16,24},{24,32},{32,40},{40,48},{48,56},{56,64},{64,7... | collective-permute-start | bytes 147464 | tf_op jit(solution)/shard_map/ppermute | solution.py:367
  28.8 1.3 %collective-permute-start.1 = (f32[48,256]{1,0:T(8,128)S(1)}, f32[48,256]{1,0:T(8,128)S(1)}, u32[]{:S(2)}, u32[]{:S(2)}) collective-permute-start(f32[48,256]{1,0:T(8,128)S(1)} %get-tuple-element.6), channel_id=1, source_target_pairs={{8,0},{16,8},{24,16},{32,24},{40,32},{48,40},{56,48},{64,56},{72,6... | collective-permute-start | bytes 147464 | tf_op jit(solution)/shard_map/ppermute | solution.py:368
  30.1 0.0 copy-done.6
  30.1 0.0 copy-done.7
  30.2 0.0 copy-done.5
  30.2 0.1 pad_add_fusion.pos
  30.3 0.4 reshape.27
  30.7 0.2 copy.17
  30.8 0.1 reshape.28.code
  31.0 0.0 collective-permute-done.up
  31.0 3.6 %collective-permute-done.1.down = f32[48,256]{1,0:T(8,128)S(1)} collective-permute-done((f32[48,256]{1,0:T(8,128)S(1)}, f32[48,256]{1,0:T(8,128)S(1)}, u32[]{:S(2)}, u32[]{:S(2)}) %collective-permute-start.1) | collective-permute-done | bytes 49184 | tf_op jit(solution)/shard_map/ppermute | solution.py:368
  34.5 12.7 %all-to-all-done.raw = f32[96,6,128]{2,1,0:T(8,128)S(1)} async-done(((f32[96,6,128]{2,1,0:T(8,128)}), f32[96,6,128]{2,1,0:T(8,128)S(1)}, u32[]{:S(2)}, u32[]{:S(2)}) %all-to-all-start) | async-done | bytes 294944 | tf_op jit(solution)/shard_map/all_to_all | solution.py:374
  47.2 2.6 %cells.1 = f32[8,64,128]{2,1,0:T(8,128)S(1)} custom-call(s32[2]{0:T(128)S(1)} %pad_add_fusion.pos, f32[120,256]{1,0:T(8,128)S(1)} %copy-done, f32[120,256]{1,0:T(8,128)S(1)} %copy-done.1, f32[120,256]{1,0:T(8,128)S(1)} %copy-done.2, f32[120,256]{1,0:T(8,128)S(1)} %copy-done.3, s32[120,256]{1,0:T(8,128)S(1)} %copy-done.4, ...), custom_call_target="tpu_custom_call" | custom-call | tf_op jit(solution)/shard_map/cells/pallas_call | solution.py:378
  49.8 14.0 %all_to_all.15.cells = f32[8,64,128]{2,1,0:T(8,128)S(1)} all-to-all(f32[8,64,128]{2,1,0:T(8,128)S(1)} %cells.1), channel_id=1, replica_groups=mesh['gy'=96,'gx'=8] {'gx'}, dimensions={0} | all-to-all | bytes 524288 | tf_op jit(solution)/shard_map/all_to_all | solution.py:381
  63.8 0.7 loads.1
  64.6 8.1 %all_to_all.16.loads = f32[8,8,128]{2,1,0:T(8,128)S(1)} all-to-all(f32[8,8,128]{2,1,0:T(8,128)S(1)} %loads.1), channel_id=1, replica_groups=mesh['gy'=96,'gx'=8] {'gx'}, dimensions={0} | all-to-all | bytes 65536 | tf_op jit(solution)/shard_map/all_to_all | solution.py:383
  72.7 5.8 %steps.1 = (f32[120,256]{1,0:T(8,128)}, f32[120,256]{1,0:T(8,128)}, f32[120,256]{1,0:T(8,128)}) custom-call(s32[2]{0:T(128)S(1)} %pad_add_fusion.pos, f32[120,256]{1,0:T(8,128)S(1)} %copy-done, f32[120,256]{1,0:T(8,128)S(1)} %copy-done.1, f32[120,256]{1,0:T(8,128)S(1)} %copy-done.2, f32[120,256]{1,0:T(8,128)S(1)} %copy-done.3, s32[120,256]{1,0:T(8,128)S(1)} %copy-done.4, ...), custom_call_target="tpu_custom_call" | custom-call | tf_op jit(solution)/shard_map/steps/pallas_call | solution.py:386
  (3 shorter events, 0.0 us)
Async XLA Ops:
  1.4 0.7 copy-start.8
  1.4 0.7 copy-start.9
  3.1 22.7 %copy-start.10 = (s32[120]{0:T(128)S(1)}, s32[120]{0:T(128)}, u32[]{:S(2)}) copy-start(s32[120]{0:T(128)} %param.17) | copy-start | bytes 1444
  3.1 22.8 %copy-start = (f32[120,256]{1,0:T(8,128)S(1)}, f32[120,256]{1,0:T(8,128)}, u32[]{:S(2)}) copy-start(f32[120,256]{1,0:T(8,128)} %eta.5) | copy-start | bytes 368644
  3.1 22.8 %copy-start.1 = (f32[120,256]{1,0:T(8,128)S(1)}, f32[120,256]{1,0:T(8,128)}, u32[]{:S(2)}) copy-start(f32[120,256]{1,0:T(8,128)} %flow_u.5) | copy-start | bytes 368644
  3.1 22.8 %copy-start.2 = (f32[120,256]{1,0:T(8,128)S(1)}, f32[120,256]{1,0:T(8,128)}, u32[]{:S(2)}) copy-start(f32[120,256]{1,0:T(8,128)} %flow_v.5) | copy-start | bytes 368644
  3.1 22.8 %copy-start.3 = (f32[120,256]{1,0:T(8,128)S(1)}, f32[120,256]{1,0:T(8,128)}, u32[]{:S(2)}) copy-start(f32[120,256]{1,0:T(8,128)} %friction.5) | copy-start | bytes 368644
  3.1 22.8 %copy-start.4 = (s32[120,256]{1,0:T(8,128)S(1)}, s32[120,256]{1,0:T(8,128)}, u32[]{:S(2)}) copy-start(s32[120,256]{1,0:T(8,128)} %levels.5) | copy-start | bytes 368644
  3.1 44.1 %all-to-all-start = ((f32[96,6,128]{2,1,0:T(8,128)}), f32[96,6,128]{2,1,0:T(8,128)S(1)}, u32[]{:S(2)}, u32[]{:S(2)}) async-start(f32[96,6,128]{2,1,0:T(8,128)} %broadcast_in_dim.12), calls=%async_computation | async-start | bytes 786432 | tf_op jit(solution)/shard_map/all_to_all | solution.py:374
  25.9 4.3 %copy-start.6 = (s32[3072]{0:T(1024)S(1)}, s32[3072]{0:T(1024)}, u32[]{:S(2)}) copy-start(s32[3072]{0:T(1024)} %param.20) | copy-start | bytes 36868
  25.9 4.3 %copy-start.7 = (s32[3072]{0:T(1024)S(1)}, s32[3072]{0:T(1024)}, u32[]{:S(2)}) copy-start(s32[3072]{0:T(1024)} %param.19) | copy-start | bytes 36868
  26.0 4.2 %copy-start.5 = (s32[3072]{0:T(1024)S(1)}, s32[3072]{0:T(1024)}, u32[]{:S(2)}) copy-start(s32[3072]{0:T(1024)} %param.21) | copy-start | bytes 36868
  26.0 5.0 %collective-permute-start = (f32[48,256]{1,0:T(8,128)S(1)}, f32[48,256]{1,0:T(8,128)S(1)}, u32[]{:S(2)}, u32[]{:S(2)}) collective-permute-start(f32[48,256]{1,0:T(8,128)S(1)} %get-tuple-element.5), channel_id=1, source_target_pairs={{0,8},{8,16},{16,24},{24,32},{32,40},{40,48},{48,56},{56,64},{64,7... | collective-permute-start | bytes 147464 | tf_op jit(solution)/shard_map/ppermute | solution.py:367
  28.8 5.7 %collective-permute-start.1 = (f32[48,256]{1,0:T(8,128)S(1)}, f32[48,256]{1,0:T(8,128)S(1)}, u32[]{:S(2)}, u32[]{:S(2)}) collective-permute-start(f32[48,256]{1,0:T(8,128)S(1)} %get-tuple-element.6), channel_id=1, source_target_pairs={{8,0},{16,8},{24,16},{32,24},{40,32},{48,40},{56,48},{64,56},{72,6... | collective-permute-start | bytes 147464 | tf_op jit(solution)/shard_map/ppermute | solution.py:368

commit v2 on v1

v2 whole, which is shorter than its diff:
```python
import functools

import jax
import jax.numpy as jnp
from jax import lax
from jax.experimental import pallas as pl
from jax.experimental.pallas import tpu as pltpu
from jax.sharding import PartitionSpec as P

SUBSTEPS = 4
LEVELS = 60

C_MASS = 0.5
C_MOMENTUM = 0.8
FRIC_STEP = 0.5
LOAD_GAIN = 0.5
FLATHER = 0.7

ROWS = 120
COLS = 256
N_GX = 8
N_GY = 96
HELD = 4
PLAT = N_GY * N_GX * HELD
COL_PLAT = N_GY * HELD

HALO = 2 * SUBSTEPS
EXT = ROWS + 2 * HALO
WIDE = COLS + 128
GROUP = 48
FIELDS = 5
SPAN = FIELDS * HALO
CELL_ROW = GROUP
STRIP_ROW = GROUP + 16
SLOT_ROWS = 72
BACK_ROWS = 8
CHUNK = 512


def iota(shape, dim):
    return lax.broadcasted_iota(jnp.int32, shape, dim)


def three_parts(x):
    high = x.astype(jnp.bfloat16).astype(jnp.float32)
    rest = x - high
    middle = rest.astype(jnp.bfloat16).astype(jnp.float32)
    return [high, middle, rest - middle]


def decode(code):
    col = jnp.bitwise_and(code, COLS - 1)
    row = jnp.bitwise_and(jnp.right_shift(code, 8), 127)
    tile_x = jnp.bitwise_and(jnp.right_shift(code, 15), N_GX - 1)
    tile_y = jnp.right_shift(code, 18)
    return tile_y, tile_x, row, col


def column_of(row_vector):
    row_vector = jnp.concatenate([row_vector, jnp.zeros((1, 128 - ROWS), jnp.float32)], axis=1)
    return jnp.transpose(jnp.broadcast_to(row_vector, (128, 128)))


def fetch(pairs, sems):
    copies = [pltpu.make_async_copy(src, dst, sems.at[n]) for n, (src, dst) in enumerate(pairs)]
    for copy in copies:
        copy.start()
    return copies


def raw_kernel(drag_in, shear_in, strip_in, slots, drag, shear, strip, sems):
    pairs = ((drag_in, drag), (shear_in, shear), (strip_in, strip))
    for copy in fetch(pairs, sems):
        copy.wait()
    held = (drag[...], shear[0], shear[1])
    lines = []
    for t in range(6):
        pieces = []
        for h in range(2):
            i = 2 * (t % 2) + h
            pieces.append(held[t // 2][i : i + 1, :])
            pieces.append(strip[h, t // 2][t % 2 : t % 2 + 1, :])
        lines.append(jnp.concatenate(pieces, axis=1))
    block = jnp.concatenate(lines, axis=0)
    for j in range(N_GY):
        slots[j] = block


def row_halo_kernel(
    eta, flow_u, flow_v, friction, levels, smap, top, bottom, low, high, sems
):
    last = ROWS - HALO
    pairs = [(levels.at[pl.ds(0, HALO), :], low), (levels.at[pl.ds(last, HALO), :], high)]
    for f, ref in enumerate((eta, flow_u, flow_v, friction)):
        part = pl.ds(f * HALO, HALO)
        pairs.append((ref.at[pl.ds(0, HALO), :], top.at[part, :]))
        pairs.append((ref.at[pl.ds(last, HALO), :], bottom.at[part, :]))
    copies = fetch(pairs, sems)
    column = column_of(smap[...].astype(jnp.float32))
    for half in (slice(0, 128), slice(128, 256)):
        top[FIELDS * HALO :, half] = column[:HALO]
        bottom[FIELDS * HALO :, half] = column[last:ROWS]
    for copy in copies:
        copy.wait()
    top[4 * HALO : 5 * HALO, :] = low[...].astype(jnp.float32)
    bottom[4 * HALO : 5 * HALO, :] = high[...].astype(jnp.float32)


def extended(f, ref, up, down):
    part = slice(f * HALO, (f + 1) * HALO)
    return jnp.concatenate([up[part, :], ref[...].astype(jnp.float32), down[part, :]], axis=0)


def cell_kernel(pos, code, *refs):
    *fields, up, down, slots = refs
    gy = pos[0]
    gx = pos[1]
    wide = [extended(f, ref, up, down) for f, ref in enumerate(fields)]
    stack = three_parts(wide[1]) + three_parts(wide[2]) + [wide[4]]
    stack.append(jnp.zeros((HALO, COLS), jnp.float32))
    table = jnp.concatenate(stack, axis=0).astype(jnp.bfloat16)
    for start in range(0, PLAT, CHUNK):
        tile_y, tile_x, row, col = decode(code[:, start : start + CHUNK])
        place = (tile_y - gy) * ROWS + row + HALO
        near = (tile_x == gx) & (place >= 0) & (place < EXT)
        hot = iota((COLS, CHUNK), 0) == jnp.where(near, col, -1)
        found = jnp.dot(
            table, hot.astype(jnp.bfloat16), preferred_element_type=jnp.float32
        )
        mine = iota((EXT, CHUNK), 0) == place
        parts = [found[n * EXT : (n + 1) * EXT] for n in range(7)]
        values = [
            parts[0] + parts[1] + parts[2],
            parts[3] + parts[4] + parts[5],
            parts[6],
        ]
        for f, value in enumerate(values):
            line = jnp.sum(jnp.where(mine, value, 0.0), axis=0, keepdims=True)
            for b in range(CHUNK // 128):
                block = start // 128 + b
                r = CELL_ROW + 3 * f + block % 3
                slots[block // 3, r : r + 1, :] = line[:, b * 128 : (b + 1) * 128]
    lane = iota((GROUP, 128), 1)
    west = jnp.zeros((GROUP, 128), jnp.float32)
    east = jnp.zeros((GROUP, 128), jnp.float32)
    for f in range(FIELDS):
        tall = jnp.concatenate(
            [wide[f], jnp.zeros((3 * GROUP - EXT, COLS), jnp.float32)], axis=0
        )
        for g in range(3):
            at = g * SPAN + f * HALO
            rows = slice(g * GROUP, (g + 1) * GROUP)
            mask = (lane >= at) & (lane < at + HALO)
            moved = pltpu.roll(tall[rows, :128], at, 1)
            west = jnp.where(mask, moved, west)
            moved = pltpu.roll(tall[rows, 128:], (at + HALO) % 128, 1)
            east = jnp.where(mask, moved, east)
    for j in range(N_GX):
        slots[j, :GROUP, :] = jnp.where(j > gx, east, west)
    for j in range(N_GX):
        slots[j, CELL_ROW + 9 :, :] = jnp.zeros((SLOT_ROWS - CELL_ROW - 9, 128), jnp.float32)


def strip_kernel(pos, raw, slots_in, slots):
    gy = pos[0]
    blocks = [raw[jnp.clip(gy - 2 + b, 0, N_GY - 1)] for b in range(5)]
    lane = iota((8, 128), 1)
    group = jnp.right_shift(jnp.bitwise_and(lane, 63), 2)
    strip = jnp.zeros((8, 128), jnp.float32)
    for t in range(6):
        lines = [block[t : t + 1, :] for block in blocks] + [jnp.zeros((3, 128), jnp.float32)]
        moved = pltpu.roll(jnp.concatenate(lines, axis=0), (4 * t - LEVELS) % 128, 1)
        strip = jnp.where(group == t, moved, strip)
    for j in range(N_GX):
        slots[j, STRIP_ROW : STRIP_ROW + 8, :] = strip


def load_kernel(cells, raw, slots):
    total = cells[0, CELL_ROW : CELL_ROW + 16, :]
    for j in range(1, N_GX):
        total = total + cells[j, CELL_ROW : CELL_ROW + 16, :]
    lines = []
    for f in range(3):
        line = jnp.concatenate([total[3 * f + q : 3 * f + q + 1, :] for q in range(3)], axis=1)
        for i in range(HELD):
            part = line[:, i * N_GY : (i + 1) * N_GY]
            lines.append(
                jnp.concatenate([part, jnp.zeros((1, 128 - N_GY), jnp.float32)], axis=1)
            )
    lines.append(jnp.zeros((128 - len(lines), 128), jnp.float32))
    columns = jnp.transpose(jnp.concatenate(lines, axis=0))[:N_GY]
    lane = iota((N_GY, 128), 1)
    low = lane < 64
    level = jnp.bitwise_and(lane, 63).astype(jnp.float32)
    result = jnp.zeros((N_GY, 128), jnp.float32)
    for q in range(2):
        u, v, wet = [
            jnp.where(
                low,
                columns[:, f * HELD + 2 * q : f * HELD + 2 * q + 1],
                columns[:, f * HELD + 2 * q + 1 : f * HELD + 2 * q + 2],
            )
            for f in range(3)
        ]
        depth = jnp.maximum(wet, 1.0) / LEVELS
        ux = u / depth + raw[:, 2 + q, :]
        uy = v / depth + raw[:, 4 + q, :]
        drag = jnp.where(level < wet, raw[:, q, :] * jnp.sqrt(ux * ux + uy * uy), 0.0)
        for c, flow in enumerate((ux, uy)):
            product = drag * flow
            for h in range(2):
                share = jnp.where(low, product, 0.0) if h == 0 else jnp.where(low, 0.0, product)
                load = jnp.sum(share, axis=1, keepdims=True) / LEVELS
                result = jnp.where(lane == c * HELD + 2 * q + h, load, result)
    result = jnp.concatenate([result, jnp.zeros((128 - N_GY, 128), jnp.float32)], axis=0)
    rows = jnp.transpose(result)
    out = []
    for c in range(2):
        line = jnp.concatenate(
            [rows[c * HELD + i : c * HELD + i + 1, :N_GY] for i in range(HELD)], axis=1
        )
        out += [line[:, q * 128 : (q + 1) * 128] for q in range(3)]
    out.append(jnp.zeros((2, 128), jnp.float32))
    block = jnp.concatenate(out, axis=0)
    for j in range(N_GX):
        slots[j] = block


def inside_of(gy, gx):
    row = iota((EXT, WIDE), 0)
    lane = iota((EXT, WIDE), 1)
    inside = ((row >= HALO) | (gy > 0)) & ((row < HALO + ROWS) | (gy < N_GY - 1))
    return inside & (
        (lane < COLS)
        | ((lane < COLS + HALO) & (gx < N_GX - 1))
        | ((lane >= WIDE - HALO) & (gx > 0))
    )


def half_step(e, u, v, rub, push, inside):
    spread = pltpu.roll(u, WIDE - 1, 1) - pltpu.roll(u, 1, 1)
    spread = spread + (pltpu.roll(v, EXT - 1, 0) - pltpu.roll(v, 1, 0))
    mid = jnp.where(inside, e - C_MASS * spread, 0.0)
    scale = 1.0 / (1.0 + rub * jnp.sqrt(u * u + v * v))
    slope_x = pltpu.roll(mid, WIDE - 1, 1) - pltpu.roll(mid, 1, 1)
    slope_y = pltpu.roll(mid, EXT - 1, 0) - pltpu.roll(mid, 1, 0)
    return mid, (u - push * slope_x) * scale, (v - push * slope_y) * scale, scale


def ready_kernel(pos, smap, cells, *refs):
    *fields, up, down, out = refs
    gy = pos[0]
    gx = pos[1]
    from_west = cells[jnp.maximum(gx - 1, 0), :GROUP, :]
    from_east = cells[jnp.minimum(gx + 1, N_GX - 1), :GROUP, :]
    lane = iota((GROUP, 128), 1)

    def widened(f, ref):
        side = []
        for g in range(3):
            at = g * SPAN + f * HALO
            east = pltpu.roll(from_east, (-at) % 128, 1)
            west = pltpu.roll(from_west, (120 - at) % 128, 1)
            side.append(jnp.where(lane < HALO, east, jnp.where(lane >= 120, west, 0.0)))
        side = jnp.concatenate(side, axis=0)[:EXT]
        return jnp.concatenate([extended(f, ref, up, down), side], axis=1)

    e, u, v, fric, lev = [widened(f, ref) for f, ref in enumerate(fields)]
    inside = inside_of(gy, gx)
    e = jnp.where(inside, e, 0.0)
    u = jnp.where(inside, u, 0.0)
    v = jnp.where(inside, v, 0.0)
    depth = jnp.where(inside, lev / LEVELS, 1.0)
    rub = jnp.where(inside, FRIC_STEP * fric / (depth * depth), 1.0)
    push = C_MOMENTUM * depth
    mid, u, v, scale = half_step(e, u, v, rub, push, inside)
    for n, field in enumerate((mid, u, v, scale, rub, push)):
        out[n] = field

    ends = FIELDS * HALO
    ids = jnp.concatenate(
        [up[ends:, :128], column_of(smap[...].astype(jnp.float32))[:ROWS], down[ends:, :128]],
        axis=0,
    ).astype(jnp.int32)
    parents = jnp.concatenate(
        [cells[j, STRIP_ROW : STRIP_ROW + 5, :] for j in range(N_GX)]
        + [jnp.zeros((128 - 5 * N_GX, 128), jnp.float32)],
        axis=0,
    )
    source = iota((EXT, 128), 1)
    column = jnp.zeros((EXT, 128), jnp.int32)
    for step in range(1, N_GX):
        column = column + (source >= 5 * step).astype(jnp.int32)
    first = ((gy - 2 + source - 5 * column) * N_GX + column) * 3
    slot_lane = jnp.right_shift(jnp.bitwise_and(iota((128, 128), 1), 63), 3)
    bound = jnp.zeros((EXT, 128), jnp.float32)
    for j in range(3):
        held = (ids == first + j) & (source < 5 * N_GX)
        for piece in three_parts(jnp.where(slot_lane == j, parents, 0.0)):
            bound = bound + jnp.dot(
                held.astype(jnp.bfloat16),
                piece.astype(jnp.bfloat16),
                preferred_element_type=jnp.float32,
            )
    bound = bound + pltpu.roll(bound, 120, 1) + pltpu.roll(bound, 112, 1)

    out[6, :, :128] = bound


def step_kernel(pos, code, loads, ready, out_eta, out_u, out_v, force):
    gy = pos[0]
    gx = pos[1]
    for start in range(0, PLAT, CHUNK):
        tile_y, tile_x, row, col = decode(code[:, start : start + CHUNK])
        place = (tile_y - gy) * ROWS + row + HALO
        across = (tile_x - gx) * COLS + col
        near = (across >= -HALO) & (across < COLS + HALO)
        across = jnp.where(near, jnp.where(across < 0, across + WIDE, across), -1)
        right = (iota((WIDE, CHUNK), 0) == across).astype(jnp.bfloat16)
        mine = iota((EXT, CHUNK), 0) == place
        left = []
        for c in range(2):
            line = jnp.concatenate(
                [
                    loads[b // 3, 3 * c + b % 3 : 3 * c + b % 3 + 1, :]
                    for b in range(start // 128, (start + CHUNK) // 128)
                ],
                axis=1,
            )
            left += [jnp.where(mine, part, 0.0) for part in three_parts(line)]
        left = jnp.concatenate(left, axis=0).astype(jnp.bfloat16)
        product = lax.dot_general(
            left,
            right,
            (((1,), (1,)), ((), ())),
            preferred_element_type=jnp.float32,
        )
        if start == 0:
            force[...] = product
        else:
            force[...] += product
    part = [force[n * EXT : (n + 1) * EXT, :] for n in range(6)]
    force_x = LOAD_GAIN * (part[0] + part[1] + part[2])
    force_y = LOAD_GAIN * (part[3] + part[4] + part[5])

    mid, flow_u, flow_v, scale, rub, push = [ready[n] for n in range(6)]
    bound = ready[6, :, :128]
    inside = inside_of(gy, gx)
    side_lane = iota((EXT, 128), 1)
    at_west = (side_lane == 0) & (gx == 0)
    at_east = (side_lane == 127) & (gx == N_GX - 1)
    root = FLATHER * jnp.sqrt(push[:, :COLS] * (1.0 / C_MOMENTUM))

    def finish(step, mid, u, v):
        sea, flow = [bound[:, 4 * f + step : 4 * f + step + 1] for f in range(2)]
        west = flow - root[:, :128] * (mid[:, :128] - sea)
        sea, flow = [bound[:, 64 + 4 * f + step : 64 + 4 * f + step + 1] for f in range(2)]
        east = flow + root[:, 128:] * (mid[:, 128:COLS] - sea)
        u = jnp.concatenate(
            [
                jnp.where(at_west, west, u[:, :128]),
                jnp.where(at_east, east, u[:, 128:COLS]),
                u[:, COLS:],
            ],
            axis=1,
        )
        return jnp.where(inside, u, 0.0), jnp.where(inside, v, 0.0)

    e = mid
    u, v = finish(0, e, flow_u - force_x * scale, flow_v - force_y * scale)
    for step in range(1, SUBSTEPS):
        e, u, v, s = half_step(e, u, v, rub, push, inside)
        u, v = finish(step, e, u - force_x * s, v - force_y * s)
    out_eta[...] = e[HALO : HALO + ROWS, :COLS]
    out_u[...] = u[HALO : HALO + ROWS, :COLS]
    out_v[...] = v[HALO : HALO + ROWS, :COLS]


def call(kernel, out_shape, spaces, name, scratch=(), limit=12, cycles=1, **kw):
    many = isinstance(out_shape, list)
    out_spec = pl.BlockSpec(memory_space=pltpu.VMEM)
    return pl.pallas_call(
        kernel,
        out_shape=out_shape,
        in_specs=[pl.BlockSpec(memory_space=space) for space in spaces],
        out_specs=[out_spec] * len(out_shape) if many else out_spec,
        scratch_shapes=list(scratch),
        compiler_params=pltpu.CompilerParams(vmem_limit_bytes=limit * 1024 * 1024),
        cost_estimate=pl.CostEstimate(
            flops=cycles * 10**8, bytes_accessed=cycles * 2 * 10**6, transcendentals=0
        ),
        name=name,
        **kw,
    )


def f32(*shape):
    return jax.ShapeDtypeStruct(shape, jnp.float32)


def on_device(
    sea_level,
    transport_x,
    transport_y,
    friction,
    levels,
    strip_map,
    parent_strip,
    plat_tile,
    plat_row,
    plat_col,
    plat_drag,
    plat_shear,
):
    pos = jnp.stack([lax.axis_index("gy"), lax.axis_index("gx")]).astype(jnp.int32)
    fields = (sea_level, transport_x, transport_y, friction, levels)
    smap = strip_map.reshape(1, ROWS)
    scalar, vmem, hbm = pltpu.SMEM, pltpu.VMEM, pltpu.HBM
    sems = pltpu.SemaphoreType.DMA

    held = call(
        raw_kernel,
        f32(N_GY, 6, 128),
        [hbm] * 3,
        "raw",
        [
            pltpu.VMEM((HELD, LEVELS), jnp.float32),
            pltpu.VMEM((2, HELD, LEVELS), jnp.float32),
            pltpu.VMEM((2, 3, 2, SUBSTEPS), jnp.float32),
            sems((3,)),
        ],
        60,
    )(plat_drag.T, plat_shear.transpose(0, 2, 1), parent_strip.transpose(0, 3, 2, 1))
    raw = lax.all_to_all(held, "gy", 0, 0, tiled=True)

    edge = pltpu.VMEM((HALO, COLS), jnp.int32)
    top, bottom = call(
        row_halo_kernel,
        [f32(GROUP, COLS), f32(GROUP, COLS)],
        [hbm] * 5 + [vmem],
        "row_halo",
        [edge, edge, sems((10,))],
        60,
    )(*fields, smap)
    count = lax.axis_size("gy")
    upward = [(i, i + 1) for i in range(count - 1)]
    downward = [(target, source) for source, target in upward]
    near = (*fields, lax.ppermute(bottom, "gy", upward), lax.ppermute(top, "gy", downward))

    code = (plat_tile << 15) | (plat_row << 8) | plat_col
    code = code.reshape(N_GY, N_GX, HELD).transpose(1, 2, 0).reshape(1, PLAT)
    slots = call(
        cell_kernel,
        f32(N_GX, SLOT_ROWS, 128),
        [scalar] + [vmem] * 8,
        "cells",
        cycles=4,
    )(pos, code, *near)
    slots = call(
        strip_kernel,
        f32(N_GX, SLOT_ROWS, 128),
        [scalar, vmem, vmem],
        "strips",
        input_output_aliases={2: 0},
    )(pos, raw, slots)
    cells = lax.all_to_all(slots, "gx", 0, 0, tiled=True)
    slots = call(load_kernel, f32(N_GX, BACK_ROWS, 128), [vmem, vmem], "loads")(cells, raw)
    loads = lax.all_to_all(slots, "gx", 0, 0, tiled=True)
    ready = call(ready_kernel, f32(7, EXT, WIDE), [scalar] + [vmem] * 9, "ready", cycles=4)(
        pos, smap, cells, *near
    )
    out = f32(ROWS, COLS)
    force = pltpu.VMEM((6 * EXT, WIDE), jnp.float32)
    return tuple(
        call(step_kernel, [out, out, out], [scalar] + [vmem] * 3, "steps", [force])(
            pos, code, loads, ready
        )
    )


def solution(mesh):
    return jax.shard_map(
        on_device,
        mesh=mesh,
        in_specs=(
            P("gy", "gx"),
            P("gy", "gx"),
            P("gy", "gx"),
            P("gy", "gx"),
            P("gy", "gx"),
            P("gy"),
            P(None, None, None, ("gy", "gx")),
            P(),
            P(),
            P(),
            P(None, ("gy", "gx")),
            P(None, None, ("gy", "gx")),
        ),
        out_specs=(P("gy", "gx"), P("gy", "gx"), P("gy", "gx")),
        check_vma=False,
    )
```

time: 78.9 us -> 77.5 us (0.982)
  blocking collectives: 22.1 us -> 14.8 us
  Pallas kernels: 9.13 us -> 14.9 us
  starting transfers between devices: 26.8 us -> 30.4 us
  local copies, waits for them, and re-layouts: 3.09 us -> 0.73 us
  waiting for transfers between devices: 16.3 us -> 15.2 us
    all_to_all x1 -> x0, blocking collectives: 8.12 us -> none  [on_device(): loads = lax.all_to_all(slots, 'gx', 0, 0, tiled=True)]
    pallas_call x4 -> x7, Pallas kernels: 9.13 us -> 14.9 us  [the longest x1 5.1 us: on_device(): call(step_kernel, [out, out, out], [scalar] + [vmem] * 3, 'steps', [force])]
    all_to_all x1 -> x2, starting transfers between devices: 22.7 us -> 26.4 us  [the longest x1 22.6 us: on_device(): raw = lax.all_to_all(held, 'gy', 0, 0, tiled=True)]
    unnamed x23 -> x18, local copies, waits for them, and re-layouts: 1.44 us -> 0.05 us
    all_to_all x1 -> x2, waiting for transfers between devices: 12.7 us -> 11.6 us  [the longest x1 8.09 us: on_device(): raw = lax.all_to_all(held, 'gy', 0, 0, tiled=True)]
    broadcast_in_dim x2 -> x0, local copies, waits for them, and re-layouts: 0.86 us -> none  [on_device(): jnp.broadcast_to(held, (N_GY, 6, 128))]
    all_to_all x1, blocking collectives: 14 us -> 14.8 us  [on_device(): cells = lax.all_to_all(slots, 'gx', 0, 0, tiled=True)]
  transfers between devices with their start and end apart: 3 -> 4, of which waited for: 2 -> 3; matrix products, arithmetic and copies ran while one was open for 1% -> 1% of each run, Pallas kernels for 0% -> 8%
where the time goes in v2:
time: 77.5 us; the launch traced here: 77 us
  starting transfers between devices  30.4 us (39%)
  waiting for transfers between devices  15.2 us (20%)
  Pallas kernels  14.9 us (19%)
  blocking collectives  14.8 us (19%)
  between operations  0.84 us (1%)
    all_to_all x1, starting transfers between devices, on_device(): raw = lax.all_to_all(held, 'gy', 0, 0, tiled=True)  22.6 us
    all_to_all x1, blocking collectives, on_device(): cells = lax.all_to_all(slots, 'gx', 0, 0, tiled=True)  14.8 us
    all_to_all x1, waiting for transfers between devices, on_device(): raw = lax.all_to_all(held, 'gy', 0, 0, tiled=True)  8.09 us
    pallas_call x1, Pallas kernels, on_device(): call(step_kernel, [out, out, out], [scalar] + [vmem] * 3, 'steps', [force])  5.1 us
    all_to_all x1, starting transfers between devices, on_device(): loads = lax.all_to_all(slots, 'gx', 0, 0, tiled=True)  3.81 us
    ppermute x1, waiting for transfers between devices, on_device(): lax.ppermute(top, 'gy', downward)  3.64 us
    all_to_all x1, waiting for transfers between devices, on_device(): loads = lax.all_to_all(slots, 'gx', 0, 0, tiled=True)  3.48 us
    ppermute x1, starting transfers between devices, on_device(): lax.ppermute(bottom, 'gy', upward)  2.7 us
  transfers between devices with their start and end apart: 4, of which 3 were waited for; matrix products, arithmetic and copies ran while one was open for 1% of the time, Pallas kernels for 8%

profile of v2, /device:TPU:1, one launch (start us, length us, event | category | flops | bytes accessed | tf_op | source)
XLA Modules:
  0.0 77.0 jit_solution(1860561609373462359)
XLA Ops:
  0.6 0.0 copy-start.4
  0.6 0.0 copy-start.3
  0.7 0.0 copy-start.2
  0.7 0.0 copy-start.1
  0.7 0.0 copy-start
  0.7 0.0 copy-start.6
  0.7 0.0 copy-start.7
  0.7 0.0 copy-start.8
  0.7 1.7 %raw.1 = f32[96,6,128]{2,1,0:T(8,128)} custom-call(f32[4,60]{1,0:T(4,128)} %bitcast.12, f32[2,4,60]{2,1,0:T(4,128)} %bitcast.11, f32[2,3,2,4]{3,2,1,0:T(2,128)} %bitcast.10), custom_call_target="tpu_custom_call" | custom-call | flops 100000000 | bytes 2000000 | tf_op jit(solution)/shard_map/raw/pallas_call | solution.py:421
  2.5 22.6 %all-to-all-start = ((f32[96,6,128]{2,1,0:T(8,128)}), f32[96,6,128]{2,1,0:T(8,128)S(1)}, u32[]{:S(2)}, u32[]{:S(2)}) async-start(f32[96,6,128]{2,1,0:T(8,128)} %raw.1), calls=%async_computation | async-start | bytes 786432 | tf_op jit(solution)/shard_map/all_to_all | solution.py:434
  25.0 2.2 %row_halo.1 = (f32[48,256]{1,0:T(8,128)}, f32[48,256]{1,0:T(8,128)}) custom-call(f32[120,256]{1,0:T(8,128)} %refs_0_.3, f32[120,256]{1,0:T(8,128)} %refs_1_.3, f32[120,256]{1,0:T(8,128)} %refs_2_.3, f32[120,256]{1,0:T(8,128)} %refs_3_.3, s32[120,256]{1,0:T(8,128)} %refs_4_.3, s32[1,120]{1,0:T(1,128)} %bitcast.7), custom_call_target="tpu_custom_call" | custom-call | flops 100000000 | bytes 2000000 | tf_op jit(solution)/shard_map/row_halo/pallas_call | solution.py:437
  27.3 2.7 %collective-permute-start = (f32[48,256]{1,0:T(8,128)}, f32[48,256]{1,0:T(8,128)S(1)}, u32[]{:S(2)}, u32[]{:S(2)}) collective-permute-start(f32[48,256]{1,0:T(8,128)} %get-tuple-element.5), channel_id=1, source_target_pairs={{0,8},{8,16},{16,24},{24,32},{32,40},{40,48},{48,56},{56,64},{64,7... | collective-permute-start | bytes 147464 | tf_op jit(solution)/shard_map/ppermute | solution.py:448
  30.0 1.3 %collective-permute-start.1 = (f32[48,256]{1,0:T(8,128)}, f32[48,256]{1,0:T(8,128)S(1)}, u32[]{:S(2)}, u32[]{:S(2)}) collective-permute-start(f32[48,256]{1,0:T(8,128)} %get-tuple-element.6), channel_id=1, source_target_pairs={{8,0},{16,8},{24,16},{32,24},{40,32},{48,40},{56,48},{64,56},{72,6... | collective-permute-start | bytes 147464 | tf_op jit(solution)/shard_map/ppermute | solution.py:448
  31.3 0.0 copy-done.6
  31.3 0.0 copy-done.7
  31.3 0.0 copy-done.8
  31.3 0.1 pad_add_fusion.pos
  31.4 0.4 reshape.15
  31.8 0.2 copy.16
  32.0 0.1 reshape.16.code
  32.1 0.0 collective-permute-done.refs_5_
  32.1 3.6 %collective-permute-done.1.refs_6_ = f32[48,256]{1,0:T(8,128)S(1)} collective-permute-done((f32[48,256]{1,0:T(8,128)}, f32[48,256]{1,0:T(8,128)S(1)}, u32[]{:S(2)}, u32[]{:S(2)}) %collective-permute-start.1) | collective-permute-done | bytes 49184 | tf_op jit(solution)/shard_map/ppermute | solution.py:448
  35.7 0.0 copy-done.4
  35.7 0.0 copy-done.3
  35.8 0.0 copy-done.2
  35.8 0.0 copy-done.1
  35.8 0.0 copy-done
  35.8 2.6 %cells.1.slots_in = f32[8,72,128]{2,1,0:T(8,128)S(1)} custom-call(s32[2]{0:T(128)S(1)} %pad_add_fusion.pos, s32[1,3072]{1,0:T(1,128)S(1)} %reshape.16.code, f32[120,256]{1,0:T(8,128)S(1)} %copy-done, f32[120,256]{1,0:T(8,128)S(1)} %copy-done.1, f32[120,256]{1,0:T(8,128)S(1)} %copy-done.2, f32[120,256]{1,0:T(8,128)S(1)} %copy-done.3, ...), custom_call_target="tpu_custom_call" | custom-call | flops 400000000 | bytes 8000000 | tf_op jit(solution)/shard_map/cells/pallas_call | solution.py:452
  38.4 0.0 copy-start.5
  38.4 8.1 %all-to-all-done.raw = f32[96,6,128]{2,1,0:T(8,128)S(1)} async-done(((f32[96,6,128]{2,1,0:T(8,128)}), f32[96,6,128]{2,1,0:T(8,128)S(1)}, u32[]{:S(2)}, u32[]{:S(2)}) %all-to-all-start) | async-done | bytes 294944 | tf_op jit(solution)/shard_map/all_to_all | solution.py:434
  46.5 0.6 strips.1
  47.1 14.8 %all_to_all.15.cells = f32[8,72,128]{2,1,0:T(8,128)S(1)} all-to-all(f32[8,72,128]{2,1,0:T(8,128)S(1)} %strips.1), channel_id=1, replica_groups=mesh['gy'=96,'gx'=8] {'gx'}, dimensions={0} | all-to-all | bytes 589824 | tf_op jit(solution)/shard_map/all_to_all | solution.py:466
  61.9 1.4 %loads.1 = f32[8,8,128]{2,1,0:T(8,128)} custom-call(f32[8,72,128]{2,1,0:T(8,128)S(1)} %all_to_all.15.cells, f32[96,6,128]{2,1,0:T(8,128)S(1)} %all-to-all-done.raw), custom_call_target="tpu_custom_call" | custom-call | flops 100000000 | bytes 2000000 | tf_op jit(solution)/shard_map/loads/pallas_call | solution.py:467
  63.3 3.8 %all-to-all-start.2 = ((f32[8,8,128]{2,1,0:T(8,128)}), f32[8,8,128]{2,1,0:T(8,128)S(1)}, u32[]{:S(2)}, u32[]{:S(2)}) async-start(f32[8,8,128]{2,1,0:T(8,128)} %loads.1), calls=%async_computation.2 | async-start | bytes 65536 | tf_op jit(solution)/shard_map/all_to_all | solution.py:468
  67.1 0.0 copy-done.5
  67.1 1.3 %ready.1 = f32[7,136,384]{2,1,0:T(8,128)S(1)} custom-call(s32[2]{0:T(128)S(1)} %pad_add_fusion.pos, s32[1,120]{1,0:T(1,128)S(1)} %bitcast.8, f32[8,72,128]{2,1,0:T(8,128)S(1)} %all_to_all.15.cells, f32[120,256]{1,0:T(8,128)S(1)} %copy-done, f32[120,256]{1,0:T(8,128)S(1)} %copy-done.1, f32[120,256]{1,0:T(8,128)S(1)} %copy-done.2, f32[120,256]{1,0:T(8,128)S(1)} %copy-done.3, ...), custom_call_target="tpu_custom_call" | custom-call | flops 400000000 | bytes 8000000 | tf_op jit(solution)/shard_map/ready/pallas_call | solution.py:469
  68.4 3.5 %all-to-all-done.2.loads = f32[8,8,128]{2,1,0:T(8,128)S(1)} async-done(((f32[8,8,128]{2,1,0:T(8,128)}), f32[8,8,128]{2,1,0:T(8,128)S(1)}, u32[]{:S(2)}, u32[]{:S(2)}) %all-to-all-start.2) | async-done | bytes 32800 | tf_op jit(solution)/shard_map/all_to_all | solution.py:468
  71.9 5.1 %steps.1 = (f32[120,256]{1,0:T(8,128)}, f32[120,256]{1,0:T(8,128)}, f32[120,256]{1,0:T(8,128)}) custom-call(s32[2]{0:T(128)S(1)} %pad_add_fusion.pos, s32[1,3072]{1,0:T(1,128)S(1)} %reshape.16.code, f32[8,8,128]{2,1,0:T(8,128)S(1)} %all-to-all-done.2.loads, f32[7,136,384]{2,1,0:T(8,128)S(1)} %ready.1), custom_call_target="tpu_custom_call" | custom-call | flops 100000000 | bytes 2000000 | tf_op jit(solution)/shard_map/steps/pallas_call | solution.py:475
  (1 shorter events, 0.0 us)
Async XLA Ops:
  0.6 35.1 %copy-start.4 = (s32[120,256]{1,0:T(8,128)S(1)}, s32[120,256]{1,0:T(8,128)}, u32[]{:S(2)}) copy-start(s32[120,256]{1,0:T(8,128)} %refs_4_.3) | copy-start | bytes 368644
  0.6 35.1 %copy-start.3 = (f32[120,256]{1,0:T(8,128)S(1)}, f32[120,256]{1,0:T(8,128)}, u32[]{:S(2)}) copy-start(f32[120,256]{1,0:T(8,128)} %refs_3_.3) | copy-start | bytes 368644
  0.7 35.1 %copy-start.2 = (f32[120,256]{1,0:T(8,128)S(1)}, f32[120,256]{1,0:T(8,128)}, u32[]{:S(2)}) copy-start(f32[120,256]{1,0:T(8,128)} %refs_2_.3) | copy-start | bytes 368644
  0.7 35.1 %copy-start.1 = (f32[120,256]{1,0:T(8,128)S(1)}, f32[120,256]{1,0:T(8,128)}, u32[]{:S(2)}) copy-start(f32[120,256]{1,0:T(8,128)} %refs_1_.3) | copy-start | bytes 368644
  0.7 35.1 %copy-start = (f32[120,256]{1,0:T(8,128)S(1)}, f32[120,256]{1,0:T(8,128)}, u32[]{:S(2)}) copy-start(f32[120,256]{1,0:T(8,128)} %refs_0_.3) | copy-start | bytes 368644
  0.7 30.6 %copy-start.6 = (s32[3072]{0:T(1024)S(1)}, s32[3072]{0:T(1024)}, u32[]{:S(2)}) copy-start(s32[3072]{0:T(1024)} %param.21) | copy-start | bytes 36868
  0.7 30.6 %copy-start.7 = (s32[3072]{0:T(1024)S(1)}, s32[3072]{0:T(1024)}, u32[]{:S(2)}) copy-start(s32[3072]{0:T(1024)} %param.20) | copy-start | bytes 36868
  0.7 30.6 %copy-start.8 = (s32[3072]{0:T(1024)S(1)}, s32[3072]{0:T(1024)}, u32[]{:S(2)}) copy-start(s32[3072]{0:T(1024)} %param.19) | copy-start | bytes 36868
  2.5 44.0 %all-to-all-start = ((f32[96,6,128]{2,1,0:T(8,128)}), f32[96,6,128]{2,1,0:T(8,128)S(1)}, u32[]{:S(2)}, u32[]{:S(2)}) async-start(f32[96,6,128]{2,1,0:T(8,128)} %raw.1), calls=%async_computation | async-start | bytes 786432 | tf_op jit(solution)/shard_map/all_to_all | solution.py:434
  27.3 4.8 %collective-permute-start = (f32[48,256]{1,0:T(8,128)}, f32[48,256]{1,0:T(8,128)S(1)}, u32[]{:S(2)}, u32[]{:S(2)}) collective-permute-start(f32[48,256]{1,0:T(8,128)} %get-tuple-element.5), channel_id=1, source_target_pairs={{0,8},{8,16},{16,24},{24,32},{32,40},{40,48},{48,56},{56,64},{64,7... | collective-permute-start | bytes 147464 | tf_op jit(solution)/shard_map/ppermute | solution.py:448
  30.0 5.8 %collective-permute-start.1 = (f32[48,256]{1,0:T(8,128)}, f32[48,256]{1,0:T(8,128)S(1)}, u32[]{:S(2)}, u32[]{:S(2)}) collective-permute-start(f32[48,256]{1,0:T(8,128)} %get-tuple-element.6), channel_id=1, source_target_pairs={{8,0},{16,8},{24,16},{32,24},{40,32},{48,40},{56,48},{64,56},{72,6... | collective-permute-start | bytes 147464 | tf_op jit(solution)/shard_map/ppermute | solution.py:448
  38.4 28.8 %copy-start.5 = (s32[120]{0:T(128)S(1)}, s32[120]{0:T(128)}, u32[]{:S(2)}) copy-start(s32[120]{0:T(128)} %param.17) | copy-start | bytes 1444
  63.3 8.6 %all-to-all-start.2 = ((f32[8,8,128]{2,1,0:T(8,128)}), f32[8,8,128]{2,1,0:T(8,128)S(1)}, u32[]{:S(2)}, u32[]{:S(2)}) async-start(f32[8,8,128]{2,1,0:T(8,128)} %loads.1), calls=%async_computation.2 | async-start | bytes 65536 | tf_op jit(solution)/shard_map/all_to_all | solution.py:468

commit v3 on v2

--- a/solution.py
+++ b/solution.py
@@ -31,10 +31,11 @@
 FIELDS = 5
 SPAN = FIELDS * HALO
 CELL_ROW = GROUP
-STRIP_ROW = GROUP + 16
-SLOT_ROWS = 72
+STRIP_ROW = GROUP + 9
+SLOT_ROWS = 64
 BACK_ROWS = 8
 CHUNK = 512
+PARTS = 3
 
 
 def iota(shape, dim):
@@ -86,24 +87,16 @@
         slots[j] = block
 
 
-def row_halo_kernel(
-    eta, flow_u, flow_v, friction, levels, smap, top, bottom, low, high, sems
-):
+def row_halo_kernel(eta, flow_u, flow_v, friction, levels, smap, top, bottom):
     last = ROWS - HALO
-    pairs = [(levels.at[pl.ds(0, HALO), :], low), (levels.at[pl.ds(last, HALO), :], high)]
-    for f, ref in enumerate((eta, flow_u, flow_v, friction)):
-        part = pl.ds(f * HALO, HALO)
-        pairs.append((ref.at[pl.ds(0, HALO), :], top.at[part, :]))
-        pairs.append((ref.at[pl.ds(last, HALO), :], bottom.at[part, :]))
-    copies = fetch(pairs, sems)
+    for f, ref in enumerate((eta, flow_u, flow_v, friction, levels)):
+        part = slice(f * HALO, (f + 1) * HALO)
+        top[part, :] = ref[:HALO, :].astype(jnp.float32)
+        bottom[part, :] = ref[last:, :].astype(jnp.float32)
     column = column_of(smap[...].astype(jnp.float32))
     for half in (slice(0, 128), slice(128, 256)):
         top[FIELDS * HALO :, half] = column[:HALO]
         bottom[FIELDS * HALO :, half] = column[last:ROWS]
-    for copy in copies:
-        copy.wait()
-    top[4 * HALO : 5 * HALO, :] = low[...].astype(jnp.float32)
-    bottom[4 * HALO : 5 * HALO, :] = high[...].astype(jnp.float32)
 
 
 def extended(f, ref, up, down):
@@ -111,10 +104,10 @@
     return jnp.concatenate([up[part, :], ref[...].astype(jnp.float32), down[part, :]], axis=0)
 
 
-def cell_kernel(pos, code, *refs):
+def cell_kernel(code, *refs):
     *fields, up, down, slots = refs
-    gy = pos[0]
-    gx = pos[1]
+    gy = lax.axis_index("gy")
+    gx = lax.axis_index("gx")
     wide = [extended(f, ref, up, down) for f, ref in enumerate(fields)]
     stack = three_parts(wide[1]) + three_parts(wide[2]) + [wide[4]]
     stack.append(jnp.zeros((HALO, COLS), jnp.float32))
@@ -161,8 +154,8 @@
         slots[j, CELL_ROW + 9 :, :] = jnp.zeros((SLOT_ROWS - CELL_ROW - 9, 128), jnp.float32)
 
 
-def strip_kernel(pos, raw, slots_in, slots):
-    gy = pos[0]
+def strip_kernel(raw, slots_in, slots):
+    gy = lax.axis_index("gy")
     blocks = [raw[jnp.clip(gy - 2 + b, 0, N_GY - 1)] for b in range(5)]
     lane = iota((8, 128), 1)
     group = jnp.right_shift(jnp.bitwise_and(lane, 63), 2)
@@ -172,13 +165,13 @@
         moved = pltpu.roll(jnp.concatenate(lines, axis=0), (4 * t - LEVELS) % 128, 1)
         strip = jnp.where(group == t, moved, strip)
     for j in range(N_GX):
-        slots[j, STRIP_ROW : STRIP_ROW + 8, :] = strip
+        slots[j, STRIP_ROW : STRIP_ROW + 5, :] = strip[:5]
 
 
 def load_kernel(cells, raw, slots):
-    total = cells[0, CELL_ROW : CELL_ROW + 16, :]
+    total = cells[0, CELL_ROW : CELL_ROW + 9, :]
     for j in range(1, N_GX):
-        total = total + cells[j, CELL_ROW : CELL_ROW + 16, :]
+        total = total + cells[j, CELL_ROW : CELL_ROW + 9, :]
     lines = []
     for f in range(3):
         line = jnp.concatenate([total[3 * f + q : 3 * f + q + 1, :] for q in range(3)], axis=1)
@@ -247,10 +240,7 @@
     return mid, (u - push * slope_x) * scale, (v - push * slope_y) * scale, scale
 
 
-def ready_kernel(pos, smap, cells, *refs):
-    *fields, up, down, out = refs
-    gy = pos[0]
-    gx = pos[1]
+def ready_for_steps(smap, cells, fields, up, down, gy, gx):
     from_west = cells[jnp.maximum(gx - 1, 0), :GROUP, :]
     from_east = cells[jnp.minimum(gx + 1, N_GX - 1), :GROUP, :]
     lane = iota((GROUP, 128), 1)
@@ -274,9 +264,6 @@
     rub = jnp.where(inside, FRIC_STEP * fric / (depth * depth), 1.0)
     push = C_MOMENTUM * depth
     mid, u, v, scale = half_step(e, u, v, rub, push, inside)
-    for n, field in enumerate((mid, u, v, scale, rub, push)):
-        out[n] = field
-
     ends = FIELDS * HALO
     ids = jnp.concatenate(
         [up[ends:, :128], column_of(smap[...].astype(jnp.float32))[:ROWS], down[ends:, :128]],
@@ -304,21 +291,24 @@
             )
     bound = bound + pltpu.roll(bound, 120, 1) + pltpu.roll(bound, 112, 1)
 
-    out[6, :, :128] = bound
-
-
-def step_kernel(pos, code, loads, ready, out_eta, out_u, out_v, force):
-    gy = pos[0]
-    gx = pos[1]
+    return mid, u, v, scale, rub, push, bound, inside
+
+
+def step_kernel(smap, code, loads, cells, *refs):
+    *fields, up, down, out_eta, out_u, out_v, force, fringe = refs
+    gy = lax.axis_index("gy")
+    gx = lax.axis_index("gx")
     for start in range(0, PLAT, CHUNK):
         tile_y, tile_x, row, col = decode(code[:, start : start + CHUNK])
         place = (tile_y - gy) * ROWS + row + HALO
+        mine = iota((EXT, CHUNK), 0) == place
         across = (tile_x - gx) * COLS + col
-        near = (across >= -HALO) & (across < COLS + HALO)
-        across = jnp.where(near, jnp.where(across < 0, across + WIDE, across), -1)
-        right = (iota((WIDE, CHUNK), 0) == across).astype(jnp.bfloat16)
-        mine = iota((EXT, CHUNK), 0) == place
+        beside = jnp.where(across < 0, across + 2 * HALO, across - COLS)
+        beside = jnp.where((across >= -HALO) & (across < COLS + HALO), beside, -1)
+        right = (iota((COLS, CHUNK), 0) == across).astype(jnp.bfloat16)
+        edge = iota((2 * HALO, CHUNK), 0) == beside
         left = []
+        side = []
         for c in range(2):
             line = jnp.concatenate(
                 [
@@ -327,25 +317,41 @@
                 ],
                 axis=1,
             )
-            left += [jnp.where(mine, part, 0.0) for part in three_parts(line)]
+            for part in three_parts(line)[:PARTS]:
+                left.append(jnp.where(mine, part, 0.0))
+                side.append(jnp.where(edge, part, 0.0))
+        side.append(jnp.zeros((128 - 2 * HALO * len(side), CHUNK), jnp.float32))
         left = jnp.concatenate(left, axis=0).astype(jnp.bfloat16)
-        product = lax.dot_general(
-            left,
-            right,
-            (((1,), (1,)), ((), ())),
-            preferred_element_type=jnp.float32,
+        side = jnp.concatenate(side, axis=0).astype(jnp.bfloat16)
+        dims = (((1,), (1,)), ((), ()))
+        inner = lax.dot_general(left, right, dims, preferred_element_type=jnp.float32)
+        outer = lax.dot_general(
+            mine.astype(jnp.bfloat16), side, dims, preferred_element_type=jnp.float32
         )
         if start == 0:
-            force[...] = product
+            force[...] = inner
+            fringe[...] = outer
         else:
-            force[...] += product
-    part = [force[n * EXT : (n + 1) * EXT, :] for n in range(6)]
-    force_x = LOAD_GAIN * (part[0] + part[1] + part[2])
-    force_y = LOAD_GAIN * (part[3] + part[4] + part[5])
-
-    mid, flow_u, flow_v, scale, rub, push = [ready[n] for n in range(6)]
-    bound = ready[6, :, :128]
-    inside = inside_of(gy, gx)
+            force[...] += inner
+            fringe[...] += outer
+    lane = iota((EXT, 128), 1)
+    sides = fringe[...]
+    forces = []
+    for c in range(2):
+        inner = force[c * PARTS * EXT : (c * PARTS + 1) * EXT, :]
+        at = 2 * HALO * PARTS * c
+        outer = pltpu.roll(sides, (-at) % 128, 1)
+        for n in range(1, PARTS):
+            inner = inner + force[(c * PARTS + n) * EXT : (c * PARTS + n + 1) * EXT, :]
+            outer = outer + pltpu.roll(sides, (-at - 2 * HALO * n) % 128, 1)
+        west = pltpu.roll(outer, 128 - 2 * HALO, 1)
+        outer = jnp.where(lane < HALO, outer, jnp.where(lane >= 128 - HALO, west, 0.0))
+        forces.append(LOAD_GAIN * jnp.concatenate([inner, outer], axis=1))
+    force_x, force_y = forces
+
+    mid, flow_u, flow_v, scale, rub, push, bound, inside = ready_for_steps(
+        smap, cells, fields, up, down, gy, gx
+    )
     side_lane = iota((EXT, 128), 1)
     at_west = (side_lane == 0) & (gx == 0)
     at_east = (side_lane == 127) & (gx == N_GX - 1)
@@ -412,10 +418,9 @@
     plat_drag,
     plat_shear,
 ):
-    pos = jnp.stack([lax.axis_index("gy"), lax.axis_index("gx")]).astype(jnp.int32)
     fields = (sea_level, transport_x, transport_y, friction, levels)
     smap = strip_map.reshape(1, ROWS)
-    scalar, vmem, hbm = pltpu.SMEM, pltpu.VMEM, pltpu.HBM
+    vmem, hbm = pltpu.VMEM, pltpu.HBM
     sems = pltpu.SemaphoreType.DMA
 
     held = call(
@@ -433,14 +438,8 @@
     )(plat_drag.T, plat_shear.transpose(0, 2, 1), parent_strip.transpose(0, 3, 2, 1))
     raw = lax.all_to_all(held, "gy", 0, 0, tiled=True)
 
-    edge = pltpu.VMEM((HALO, COLS), jnp.int32)
     top, bottom = call(
-        row_halo_kernel,
-        [f32(GROUP, COLS), f32(GROUP, COLS)],
-        [hbm] * 5 + [vmem],
-        "row_halo",
-        [edge, edge, sems((10,))],
-        60,
+        row_halo_kernel, [f32(GROUP, COLS), f32(GROUP, COLS)], [vmem] * 6, "row_halo"
     )(*fields, smap)
     count = lax.axis_size("gy")
     upward = [(i, i + 1) for i in range(count - 1)]
@@ -452,28 +451,28 @@
     slots = call(
         cell_kernel,
         f32(N_GX, SLOT_ROWS, 128),
-        [scalar] + [vmem] * 8,
+        [vmem] * 8,
         "cells",
         cycles=4,
-    )(pos, code, *near)
+    )(code, *near)
     slots = call(
         strip_kernel,
         f32(N_GX, SLOT_ROWS, 128),
-        [scalar, vmem, vmem],
+        [vmem, vmem],
         "strips",
-        input_output_aliases={2: 0},
-    )(pos, raw, slots)
+        input_output_aliases={1: 0},
+    )(raw, slots)
     cells = lax.all_to_all(slots, "gx", 0, 0, tiled=True)
     slots = call(load_kernel, f32(N_GX, BACK_ROWS, 128), [vmem, vmem], "loads")(cells, raw)
     loads = lax.all_to_all(slots, "gx", 0, 0, tiled=True)
-    ready = call(ready_kernel, f32(7, EXT, WIDE), [scalar] + [vmem] * 9, "ready", cycles=4)(
-        pos, smap, cells, *near
-    )
     out = f32(ROWS, COLS)
-    force = pltpu.VMEM((6 * EXT, WIDE), jnp.float32)
+    force = [
+        pltpu.VMEM((2 * PARTS * EXT, COLS), jnp.float32),
+        pltpu.VMEM((EXT, 128), jnp.float32),
+    ]
     return tuple(
-        call(step_kernel, [out, out, out], [scalar] + [vmem] * 3, "steps", [force])(
-            pos, code, loads, ready
+        call(step_kernel, [out, out, out], [vmem] * 11, "steps", force)(
+            smap, code, loads, cells, *near
         )
     )
 

time: 77.5 us -> 74.1 us (0.956)
  blocking collectives: 14.8 us -> 22.1 us
  Pallas kernels: 14.9 us -> 8.88 us
  starting transfers between devices: 30.4 us -> 26.7 us
  waiting for transfers between devices: 15.2 us -> 13.9 us
    all_to_all x0 -> x1, blocking collectives: none -> 8.12 us  [on_device(): loads = lax.all_to_all(slots, 'gx', 0, 0, tiled=True)]
    pallas_call x5 -> x4, Pallas kernels: 11.8 us -> 6.53 us  [the longest x1 4.35 us: on_device(): call(step_kernel, [out, out, out], [vmem] * 11, 'steps', force)]
    all_to_all x1 -> x0, starting transfers between devices: 3.81 us -> none  [on_device(): loads = lax.all_to_all(slots, 'gx', 0, 0, tiled=True)]
    all_to_all x1 -> x0, waiting for transfers between devices: 3.48 us -> none  [on_device(): loads = lax.all_to_all(slots, 'gx', 0, 0, tiled=True)]
    all_to_all x1, waiting for transfers between devices: 8.09 us -> 10.3 us  [on_device(): raw = lax.all_to_all(held, 'gy', 0, 0, tiled=True)]
    all_to_all x1, blocking collectives: 14.8 us -> 14 us  [on_device(): cells = lax.all_to_all(slots, 'gx', 0, 0, tiled=True)]
  transfers between devices with their start and end apart: 4 -> 3, of which waited for: 3 -> 2; matrix products, arithmetic and copies ran while one was open for 1% -> 1% of each run, Pallas kernels for 8% -> 3%
where the time goes in v3:
time: 74.1 us; the launch traced here: 73.8 us
  starting transfers between devices  26.7 us (36%)
  blocking collectives  22.1 us (30%)
  waiting for transfers between devices  13.9 us (19%)
  Pallas kernels  8.88 us (12%)
  local copies, waits for them, and re-layouts  1.32 us (2%)
  between operations  0.82 us (1%)
    all_to_all x1, starting transfers between devices, on_device(): raw = lax.all_to_all(held, 'gy', 0, 0, tiled=True)  22.7 us
    all_to_all x1, blocking collectives, on_device(): cells = lax.all_to_all(slots, 'gx', 0, 0, tiled=True)  14 us
    all_to_all x1, waiting for transfers between devices, on_device(): raw = lax.all_to_all(held, 'gy', 0, 0, tiled=True)  10.3 us
    all_to_all x1, blocking collectives, on_device(): loads = lax.all_to_all(slots, 'gx', 0, 0, tiled=True)  8.12 us
    pallas_call x1, Pallas kernels, on_device(): call(step_kernel, [out, out, out], [vmem] * 11, 'steps', force)  4.35 us
    ppermute x1, waiting for transfers between devices, on_device(): lax.ppermute(top, 'gy', downward)  3.6 us
    ppermute x1, starting transfers between devices, on_device(): lax.ppermute(bottom, 'gy', upward)  2.73 us
    pallas_call x1, Pallas kernels, on_device(): call(cell_kernel, f32(N_GX, SLOT_ROWS, 128), [vmem] * 8, 'cells', cycles=4)  2.02 us
  transfers between devices with their start and end apart: 3, of which 2 were waited for; matrix products, arithmetic and copies ran while one was open for 1% of the time, Pallas kernels for 3%

profile of v3, /device:TPU:1, one launch (start us, length us, event | category | flops | bytes accessed | tf_op | source)
XLA Modules:
  0.0 73.8 jit_solution(6072361623240276689)
XLA Ops:
  0.6 1.6 %raw.1 = f32[96,6,128]{2,1,0:T(8,128)} custom-call(f32[4,60]{1,0:T(4,128)} %bitcast.10, f32[2,4,60]{2,1,0:T(4,128)} %bitcast.9, f32[2,3,2,4]{3,2,1,0:T(2,128)} %bitcast.8), custom_call_target="tpu_custom_call" | custom-call | flops 100000000 | bytes 2000000 | tf_op jit(solution)/shard_map/raw/pallas_call | solution.py:426
  2.2 0.0 copy-start
  2.3 0.0 copy-start.1
  2.3 0.0 copy-start.2
  2.3 0.0 copy-start.3
  2.3 0.0 copy-start.4
  2.3 22.7 %all-to-all-start = ((f32[96,6,128]{2,1,0:T(8,128)}), f32[96,6,128]{2,1,0:T(8,128)S(1)}, u32[]{:S(2)}, u32[]{:S(2)}) async-start(f32[96,6,128]{2,1,0:T(8,128)} %raw.1), calls=%async_computation | async-start | bytes 786432 | tf_op jit(solution)/shard_map/all_to_all | solution.py:439
  25.0 0.0 copy-start.5
  25.0 0.0 copy-done
  25.0 0.0 copy-done.1
  25.0 0.0 copy-done.2
  25.0 0.0 copy-done.3
  25.1 0.0 copy-done.4
  25.1 0.6 copy-done.5
  25.7 0.0 copy-start.6
  25.7 0.0 copy-start.7
  25.7 0.0 copy-start.8
  25.7 0.1 row_halo.1
  25.7 2.7 %collective-permute-start = (f32[48,256]{1,0:T(8,128)S(1)}, f32[48,256]{1,0:T(8,128)S(1)}, u32[]{:S(2)}, u32[]{:S(2)}) collective-permute-start(f32[48,256]{1,0:T(8,128)S(1)} %get-tuple-element.5), channel_id=1, source_target_pairs={{0,8},{8,16},{16,24},{24,32},{32,40},{40,48},{48,56},{56,64},{64,7... | collective-permute-start | bytes 147464 | tf_op jit(solution)/shard_map/ppermute | solution.py:447
  28.5 1.3 %collective-permute-start.1 = (f32[48,256]{1,0:T(8,128)S(1)}, f32[48,256]{1,0:T(8,128)S(1)}, u32[]{:S(2)}, u32[]{:S(2)}) collective-permute-start(f32[48,256]{1,0:T(8,128)S(1)} %get-tuple-element.6), channel_id=1, source_target_pairs={{8,0},{16,8},{24,16},{32,24},{40,32},{48,40},{56,48},{64,56},{72,6... | collective-permute-start | bytes 147464 | tf_op jit(solution)/shard_map/ppermute | solution.py:447
  29.8 0.0 copy-done.6
  29.8 0.0 copy-done.7
  29.8 0.0 copy-done.8
  29.8 0.4 reshape.16
  30.2 0.2 copy.16
  30.4 0.1 reshape.17.code
  30.5 0.0 collective-permute-done.refs_5_
  30.5 3.6 %collective-permute-done.1.refs_6_ = f32[48,256]{1,0:T(8,128)S(1)} collective-permute-done((f32[48,256]{1,0:T(8,128)S(1)}, f32[48,256]{1,0:T(8,128)S(1)}, u32[]{:S(2)}, u32[]{:S(2)}) %collective-permute-start.1) | collective-permute-done | bytes 49184 | tf_op jit(solution)/shard_map/ppermute | solution.py:447
  34.1 2.0 %cells.1.slots_in = f32[8,64,128]{2,1,0:T(8,128)S(1)} custom-call(s32[1,3072]{1,0:T(1,128)S(1)} %reshape.17.code, f32[120,256]{1,0:T(8,128)S(1)} %copy-done, f32[120,256]{1,0:T(8,128)S(1)} %copy-done.1, f32[120,256]{1,0:T(8,128)S(1)} %copy-done.2, f32[120,256]{1,0:T(8,128)S(1)} %copy-done.3, s32[120,256]{1,0:T(8,128)S(1)} %copy-done.4, ...), custom_call_target="tpu_custom_call" | custom-call | flops 400000000 | bytes 8000000 | tf_op jit(solution)/shard_map/cells/pallas_call | solution.py:451
  36.1 10.3 %all-to-all-done.raw = f32[96,6,128]{2,1,0:T(8,128)S(1)} async-done(((f32[96,6,128]{2,1,0:T(8,128)}), f32[96,6,128]{2,1,0:T(8,128)S(1)}, u32[]{:S(2)}, u32[]{:S(2)}) %all-to-all-start) | async-done | bytes 294944 | tf_op jit(solution)/shard_map/all_to_all | solution.py:439
  46.4 0.1 strips.1
  46.5 14.0 %all_to_all.15.cells = f32[8,64,128]{2,1,0:T(8,128)S(1)} all-to-all(f32[8,64,128]{2,1,0:T(8,128)S(1)} %strips.1), channel_id=1, replica_groups=mesh['gy'=96,'gx'=8] {'gx'}, dimensions={0} | all-to-all | bytes 524288 | tf_op jit(solution)/shard_map/all_to_all | solution.py:465
  60.5 0.8 %loads.1 = f32[8,8,128]{2,1,0:T(8,128)S(1)} custom-call(f32[8,64,128]{2,1,0:T(8,128)S(1)} %all_to_all.15.cells, f32[96,6,128]{2,1,0:T(8,128)S(1)} %all-to-all-done.raw), custom_call_target="tpu_custom_call" | custom-call | flops 100000000 | bytes 2000000 | tf_op jit(solution)/shard_map/loads/pallas_call | solution.py:466
  61.3 8.1 %all_to_all.16.loads = f32[8,8,128]{2,1,0:T(8,128)S(1)} all-to-all(f32[8,8,128]{2,1,0:T(8,128)S(1)} %loads.1), channel_id=1, replica_groups=mesh['gy'=96,'gx'=8] {'gx'}, dimensions={0} | all-to-all | bytes 65536 | tf_op jit(solution)/shard_map/all_to_all | solution.py:467
  69.4 4.4 %steps.1 = (f32[120,256]{1,0:T(8,128)}, f32[120,256]{1,0:T(8,128)}, f32[120,256]{1,0:T(8,128)}) custom-call(s32[1,120]{1,0:T(1,128)S(1)} %bitcast.6, s32[1,3072]{1,0:T(1,128)S(1)} %reshape.17.code, f32[8,8,128]{2,1,0:T(8,128)S(1)} %all_to_all.16.loads, f32[8,64,128]{2,1,0:T(8,128)S(1)} %all_to_all.15.cells, f32[120,256]{1,0:T(8,128)S(1)} %copy-done, ...), custom_call_target="tpu_custom_call" | custom-call | flops 100000000 | bytes 2000000 | tf_op jit(solution)/shard_map/steps/pallas_call | solution.py:474
  (1 shorter events, 0.0 us)
Async XLA Ops:
  2.2 22.8 %copy-start = (f32[120,256]{1,0:T(8,128)S(1)}, f32[120,256]{1,0:T(8,128)}, u32[]{:S(2)}) copy-start(f32[120,256]{1,0:T(8,128)} %refs_0_.3) | copy-start | bytes 368644
  2.3 22.8 %copy-start.1 = (f32[120,256]{1,0:T(8,128)S(1)}, f32[120,256]{1,0:T(8,128)}, u32[]{:S(2)}) copy-start(f32[120,256]{1,0:T(8,128)} %refs_1_.3) | copy-start | bytes 368644
  2.3 22.8 %copy-start.2 = (f32[120,256]{1,0:T(8,128)S(1)}, f32[120,256]{1,0:T(8,128)}, u32[]{:S(2)}) copy-start(f32[120,256]{1,0:T(8,128)} %refs_2_.3) | copy-start | bytes 368644
  2.3 22.8 %copy-start.3 = (f32[120,256]{1,0:T(8,128)S(1)}, f32[120,256]{1,0:T(8,128)}, u32[]{:S(2)}) copy-start(f32[120,256]{1,0:T(8,128)} %refs_3_.3) | copy-start | bytes 368644
  2.3 22.8 %copy-start.4 = (s32[120,256]{1,0:T(8,128)S(1)}, s32[120,256]{1,0:T(8,128)}, u32[]{:S(2)}) copy-start(s32[120,256]{1,0:T(8,128)} %refs_4_.3) | copy-start | bytes 368644
  2.3 44.1 %all-to-all-start = ((f32[96,6,128]{2,1,0:T(8,128)}), f32[96,6,128]{2,1,0:T(8,128)S(1)}, u32[]{:S(2)}, u32[]{:S(2)}) async-start(f32[96,6,128]{2,1,0:T(8,128)} %raw.1), calls=%async_computation | async-start | bytes 786432 | tf_op jit(solution)/shard_map/all_to_all | solution.py:439
  25.0 0.7 copy-start.5
  25.7 4.1 %copy-start.6 = (s32[3072]{0:T(1024)S(1)}, s32[3072]{0:T(1024)}, u32[]{:S(2)}) copy-start(s32[3072]{0:T(1024)} %param.21) | copy-start | bytes 36868
  25.7 4.1 %copy-start.7 = (s32[3072]{0:T(1024)S(1)}, s32[3072]{0:T(1024)}, u32[]{:S(2)}) copy-start(s32[3072]{0:T(1024)} %param.20) | copy-start | bytes 36868
  25.7 4.1 %copy-start.8 = (s32[3072]{0:T(1024)S(1)}, s32[3072]{0:T(1024)}, u32[]{:S(2)}) copy-start(s32[3072]{0:T(1024)} %param.19) | copy-start | bytes 36868
  25.7 4.8 %collective-permute-start = (f32[48,256]{1,0:T(8,128)S(1)}, f32[48,256]{1,0:T(8,128)S(1)}, u32[]{:S(2)}, u32[]{:S(2)}) collective-permute-start(f32[48,256]{1,0:T(8,128)S(1)} %get-tuple-element.5), channel_id=1, source_target_pairs={{0,8},{8,16},{16,24},{24,32},{32,40},{40,48},{48,56},{56,64},{64,7... | collective-permute-start | bytes 147464 | tf_op jit(solution)/shard_map/ppermute | solution.py:447
  28.5 5.7 %collective-permute-start.1 = (f32[48,256]{1,0:T(8,128)S(1)}, f32[48,256]{1,0:T(8,128)S(1)}, u32[]{:S(2)}, u32[]{:S(2)}) collective-permute-start(f32[48,256]{1,0:T(8,128)S(1)} %get-tuple-element.6), channel_id=1, source_target_pairs={{8,0},{16,8},{24,16},{32,24},{40,32},{48,40},{56,48},{64,56},{72,6... | collective-permute-start | bytes 147464 | tf_op jit(solution)/shard_map/ppermute | solution.py:447

commit v4 on v3

--- a/solution.py
+++ b/solution.py
@@ -35,11 +35,24 @@
 SLOT_ROWS = 64
 BACK_ROWS = 8
 CHUNK = 512
+FIRST_ROW = 68
+FIRST_COL = 5
+ROW_GROUP = [[(n + FIRST_ROW) % N_GY for n in range(N_GY)]]
+COL_GROUP = [[(n + FIRST_COL) % N_GX for n in range(N_GX)]]
 PARTS = 3
 
 
 def iota(shape, dim):
     return lax.broadcasted_iota(jnp.int32, shape, dim)
+
+
+def row_slot(gy):
+    return lax.rem(gy + (N_GY - FIRST_ROW), N_GY)
+
+
+def col_slot(gx):
+    gx = gx + (N_GX - FIRST_COL)
+    return gx % N_GX if isinstance(gx, int) else lax.rem(gx, N_GX)
 
 
 def three_parts(x):
@@ -132,7 +145,7 @@
             for b in range(CHUNK // 128):
                 block = start // 128 + b
                 r = CELL_ROW + 3 * f + block % 3
-                slots[block // 3, r : r + 1, :] = line[:, b * 128 : (b + 1) * 128]
+                slots[col_slot(block // 3), r : r + 1, :] = line[:, b * 128 : (b + 1) * 128]
     lane = iota((GROUP, 128), 1)
     west = jnp.zeros((GROUP, 128), jnp.float32)
     east = jnp.zeros((GROUP, 128), jnp.float32)
@@ -149,14 +162,14 @@
             moved = pltpu.roll(tall[rows, 128:], (at + HALO) % 128, 1)
             east = jnp.where(mask, moved, east)
     for j in range(N_GX):
-        slots[j, :GROUP, :] = jnp.where(j > gx, east, west)
+        slots[col_slot(j), :GROUP, :] = jnp.where(j > gx, east, west)
     for j in range(N_GX):
         slots[j, CELL_ROW + 9 :, :] = jnp.zeros((SLOT_ROWS - CELL_ROW - 9, 128), jnp.float32)
 
 
 def strip_kernel(raw, slots_in, slots):
     gy = lax.axis_index("gy")
-    blocks = [raw[jnp.clip(gy - 2 + b, 0, N_GY - 1)] for b in range(5)]
+    blocks = [raw[row_slot(jnp.clip(gy - 2 + b, 0, N_GY - 1))] for b in range(5)]
     lane = iota((8, 128), 1)
     group = jnp.right_shift(jnp.bitwise_and(lane, 63), 2)
     strip = jnp.zeros((8, 128), jnp.float32)
@@ -241,8 +254,8 @@
 
 
 def ready_for_steps(smap, cells, fields, up, down, gy, gx):
-    from_west = cells[jnp.maximum(gx - 1, 0), :GROUP, :]
-    from_east = cells[jnp.minimum(gx + 1, N_GX - 1), :GROUP, :]
+    from_west = cells[col_slot(jnp.maximum(gx - 1, 0)), :GROUP, :]
+    from_east = cells[col_slot(jnp.minimum(gx + 1, N_GX - 1)), :GROUP, :]
     lane = iota((GROUP, 128), 1)
 
     def widened(f, ref):
@@ -270,7 +283,7 @@
         axis=0,
     ).astype(jnp.int32)
     parents = jnp.concatenate(
-        [cells[j, STRIP_ROW : STRIP_ROW + 5, :] for j in range(N_GX)]
+        [cells[col_slot(j), STRIP_ROW : STRIP_ROW + 5, :] for j in range(N_GX)]
         + [jnp.zeros((128 - 5 * N_GX, 128), jnp.float32)],
         axis=0,
     )
@@ -312,7 +325,7 @@
         for c in range(2):
             line = jnp.concatenate(
                 [
-                    loads[b // 3, 3 * c + b % 3 : 3 * c + b % 3 + 1, :]
+                    loads[col_slot(b // 3), 3 * c + b % 3 : 3 * c + b % 3 + 1, :]
                     for b in range(start // 128, (start + CHUNK) // 128)
                 ],
                 axis=1,
@@ -436,7 +449,9 @@
         ],
         60,
     )(plat_drag.T, plat_shear.transpose(0, 2, 1), parent_strip.transpose(0, 3, 2, 1))
-    raw = lax.all_to_all(held, "gy", 0, 0, tiled=True)
+    raw = lax.all_to_all(
+        held, "gy", 0, 0, axis_index_groups=ROW_GROUP, tiled=True
+    )
 
     top, bottom = call(
         row_halo_kernel, [f32(GROUP, COLS), f32(GROUP, COLS)], [vmem] * 6, "row_halo"
@@ -447,7 +462,8 @@
     near = (*fields, lax.ppermute(bottom, "gy", upward), lax.ppermute(top, "gy", downward))
 
     code = (plat_tile << 15) | (plat_row << 8) | plat_col
-    code = code.reshape(N_GY, N_GX, HELD).transpose(1, 2, 0).reshape(1, PLAT)
+    start = FIRST_ROW * N_GX * HELD
+    code = jnp.concatenate([code[start:], code[:start]]).reshape(N_GY, N_GX, HELD).transpose(1, 2, 0).reshape(1, PLAT)
     slots = call(
         cell_kernel,
         f32(N_GX, SLOT_ROWS, 128),
@@ -462,9 +478,9 @@
         "strips",
         input_output_aliases={1: 0},
     )(raw, slots)
-    cells = lax.all_to_all(slots, "gx", 0, 0, tiled=True)
+    cells = lax.all_to_all(slots, "gx", 0, 0, axis_index_groups=COL_GROUP, tiled=True)
     slots = call(load_kernel, f32(N_GX, BACK_ROWS, 128), [vmem, vmem], "loads")(cells, raw)
-    loads = lax.all_to_all(slots, "gx", 0, 0, tiled=True)
+    loads = lax.all_to_all(slots, "gx", 0, 0, axis_index_groups=COL_GROUP, tiled=True)
     out = f32(ROWS, COLS)
     force = [
         pltpu.VMEM((2 * PARTS * EXT, COLS), jnp.float32),

time: 74.1 us -> 64.8 us (0.87)
  waiting for transfers between devices: 13.9 us -> 7.73 us
  blocking collectives: 22.1 us -> 17.9 us
  starting transfers between devices: 26.7 us -> 27.8 us
    all_to_all x1, waiting for transfers between devices: 10.3 us -> 3.45 us  [on_device(): lax.all_to_all(held, 'gy', 0, 0, axis_index_groups=ROW_GROUP, tiled=True)]
    all_to_all x2, blocking collectives: 22.1 us -> 17.9 us  [on_device(): lax.all_to_all(slots, 'gx', 0, 0, axis_index_groups=COL_GROUP, tiled=True)]
    all_to_all x1, starting transfers between devices: 22.7 us -> 24.2 us  [on_device(): lax.all_to_all(held, 'gy', 0, 0, axis_index_groups=ROW_GROUP, tiled=True)]
where the time goes in v4:
time: 64.8 us; the launch traced here: 64.4 us
  starting transfers between devices  27.8 us (43%)
  blocking collectives  17.9 us (28%)
  Pallas kernels  8.87 us (14%)
  waiting for transfers between devices  7.73 us (12%)
  local copies, waits for them, and re-layouts  1.33 us (2%)
  between operations  0.83 us (1%)
    all_to_all x1, starting transfers between devices, on_device(): lax.all_to_all(held, 'gy', 0, 0, axis_index_groups=ROW_GROUP, tiled=True)  24.2 us
    all_to_all x2, blocking collectives, on_device(): lax.all_to_all(slots, 'gx', 0, 0, axis_index_groups=COL_GROUP, tiled=True)  17.9 us
    pallas_call x1, Pallas kernels, on_device(): call(step_kernel, [out, out, out], [vmem] * 11, 'steps', force)  4.35 us
    ppermute x1, waiting for transfers between devices, on_device(): lax.ppermute(top, 'gy', downward)  4.28 us
    all_to_all x1, waiting for transfers between devices, on_device(): lax.all_to_all(held, 'gy', 0, 0, axis_index_groups=ROW_GROUP, tiled=True)  3.45 us
    ppermute x1, starting transfers between devices, on_device(): lax.ppermute(bottom, 'gy', upward)  2.23 us
    pallas_call x1, Pallas kernels, on_device(): call(cell_kernel, f32(N_GX, SLOT_ROWS, 128), [vmem] * 8, 'cells', cycles=4)  2.02 us
    pallas_call x1, Pallas kernels, on_device(): call(raw_kernel, f32(N_GY, 6, 128), [hbm] * 3, 'raw', [pltpu.VMEM((HELD,...  1.6 us
  transfers between devices with their start and end apart: 3, of which 2 were waited for; matrix products, arithmetic and copies ran while one was open for 1% of the time, Pallas kernels for 3%

profile of v4, /device:TPU:1, one launch (start us, length us, event | category | flops | bytes accessed | tf_op | source)
XLA Modules:
  0.0 64.4 jit_solution(17261684908801213652)
XLA Ops:
  0.6 1.6 %raw.1 = f32[96,6,128]{2,1,0:T(8,128)} custom-call(f32[4,60]{1,0:T(4,128)} %bitcast.12, f32[2,4,60]{2,1,0:T(4,128)} %bitcast.11, f32[2,3,2,4]{3,2,1,0:T(2,128)} %bitcast.10), custom_call_target="tpu_custom_call" | custom-call | flops 100000000 | bytes 2000000 | tf_op jit(solution)/shard_map/raw/pallas_call | solution.py:439
  2.2 0.0 copy-start
  2.3 0.0 copy-start.1
  2.3 0.0 copy-start.2
  2.3 0.0 copy-start.3
  2.3 0.0 copy-start.4
  2.3 24.2 %all-to-all-start = ((f32[96,6,128]{2,1,0:T(8,128)}), f32[96,6,128]{2,1,0:T(8,128)S(1)}, u32[]{:S(2)}, u32[]{:S(2)}) async-start(f32[96,6,128]{2,1,0:T(8,128)} %raw.1), calls=%async_computation | async-start | bytes 786432 | tf_op jit(solution)/shard_map/all_to_all | solution.py:452
  26.5 0.0 copy-start.5
  26.6 0.0 copy-done
  26.6 0.0 copy-done.1
  26.6 0.0 copy-done.2
  26.6 0.0 copy-done.3
  26.6 0.0 copy-done.4
  26.6 0.6 copy-done.5
  27.2 0.0 copy-start.6
  27.2 0.0 copy-start.7
  27.2 0.0 copy-start.8
  27.2 0.1 row_halo.1
  27.3 2.2 %collective-permute-start = (f32[48,256]{1,0:T(8,128)S(1)}, f32[48,256]{1,0:T(8,128)S(1)}, u32[]{:S(2)}, u32[]{:S(2)}) collective-permute-start(f32[48,256]{1,0:T(8,128)S(1)} %get-tuple-element.5), channel_id=1, source_target_pairs={{0,8},{8,16},{16,24},{24,32},{32,40},{40,48},{48,56},{56,64},{64,7... | collective-permute-start | bytes 147464 | tf_op jit(solution)/shard_map/ppermute | solution.py:462
  29.5 1.3 %collective-permute-start.1 = (f32[48,256]{1,0:T(8,128)S(1)}, f32[48,256]{1,0:T(8,128)S(1)}, u32[]{:S(2)}, u32[]{:S(2)}) collective-permute-start(f32[48,256]{1,0:T(8,128)S(1)} %get-tuple-element.6), channel_id=1, source_target_pairs={{8,0},{16,8},{24,16},{32,24},{40,32},{48,40},{56,48},{64,56},{72,6... | collective-permute-start | bytes 147464 | tf_op jit(solution)/shard_map/ppermute | solution.py:462
  30.8 0.0 copy-done.6
  30.8 0.0 copy-done.7
  30.8 0.0 copy-done.8
  30.9 0.4 reshape.16
  31.3 0.2 copy.16
  31.5 0.1 reshape.17.code
  31.6 0.0 collective-permute-done.refs_5_
  31.6 4.3 %collective-permute-done.1.refs_6_ = f32[48,256]{1,0:T(8,128)S(1)} collective-permute-done((f32[48,256]{1,0:T(8,128)S(1)}, f32[48,256]{1,0:T(8,128)S(1)}, u32[]{:S(2)}, u32[]{:S(2)}) %collective-permute-start.1) | collective-permute-done | bytes 49184 | tf_op jit(solution)/shard_map/ppermute | solution.py:462
  35.9 2.0 %cells.1.slots_in = f32[8,64,128]{2,1,0:T(8,128)S(1)} custom-call(s32[1,3072]{1,0:T(1,128)S(1)} %reshape.17.code, f32[120,256]{1,0:T(8,128)S(1)} %copy-done, f32[120,256]{1,0:T(8,128)S(1)} %copy-done.1, f32[120,256]{1,0:T(8,128)S(1)} %copy-done.2, f32[120,256]{1,0:T(8,128)S(1)} %copy-done.3, s32[120,256]{1,0:T(8,128)S(1)} %copy-done.4, ...), custom_call_target="tpu_custom_call" | custom-call | flops 400000000 | bytes 8000000 | tf_op jit(solution)/shard_map/cells/pallas_call | solution.py:467
  37.9 3.4 %all-to-all-done.raw = f32[96,6,128]{2,1,0:T(8,128)S(1)} async-done(((f32[96,6,128]{2,1,0:T(8,128)}), f32[96,6,128]{2,1,0:T(8,128)S(1)}, u32[]{:S(2)}, u32[]{:S(2)}) %all-to-all-start) | async-done | bytes 294944 | tf_op jit(solution)/shard_map/all_to_all | solution.py:452
  41.3 0.1 strips.1
  41.4 10.0 %all_to_all.15.cells = f32[8,64,128]{2,1,0:T(8,128)S(1)} all-to-all(f32[8,64,128]{2,1,0:T(8,128)S(1)} %strips.1), channel_id=1, replica_groups={{5,6,7,0,1,2,3,4},{13,14,15,8,9,10,11,12},{21,22,23,16,17,18,19,20},{29..., dimensions={0} | all-to-all | bytes 524288 | tf_op jit(solution)/shard_map/all_to_all | solution.py:481
  51.4 0.8 %loads.1 = f32[8,8,128]{2,1,0:T(8,128)S(1)} custom-call(f32[8,64,128]{2,1,0:T(8,128)S(1)} %all_to_all.15.cells, f32[96,6,128]{2,1,0:T(8,128)S(1)} %all-to-all-done.raw), custom_call_target="tpu_custom_call" | custom-call | flops 100000000 | bytes 2000000 | tf_op jit(solution)/shard_map/loads/pallas_call | solution.py:482
  52.2 7.9 %all_to_all.16.loads = f32[8,8,128]{2,1,0:T(8,128)S(1)} all-to-all(f32[8,8,128]{2,1,0:T(8,128)S(1)} %loads.1), channel_id=1, replica_groups={{5,6,7,0,1,2,3,4},{13,14,15,8,9,10,11,12},{21,22,23,16,17,18,19,20},{29..., dimensions={0} | all-to-all | bytes 65536 | tf_op jit(solution)/shard_map/all_to_all | solution.py:483
  60.0 4.3 %steps.1 = (f32[120,256]{1,0:T(8,128)}, f32[120,256]{1,0:T(8,128)}, f32[120,256]{1,0:T(8,128)}) custom-call(s32[1,120]{1,0:T(1,128)S(1)} %bitcast.7, s32[1,3072]{1,0:T(1,128)S(1)} %reshape.17.code, f32[8,8,128]{2,1,0:T(8,128)S(1)} %all_to_all.16.loads, f32[8,64,128]{2,1,0:T(8,128)S(1)} %all_to_all.15.cells, f32[120,256]{1,0:T(8,128)S(1)} %copy-done, ...), custom_call_target="tpu_custom_call" | custom-call | flops 100000000 | bytes 2000000 | tf_op jit(solution)/shard_map/steps/pallas_call | solution.py:490
  (3 shorter events, 0.0 us)
Async XLA Ops:
  2.2 24.3 %copy-start = (f32[120,256]{1,0:T(8,128)S(1)}, f32[120,256]{1,0:T(8,128)}, u32[]{:S(2)}) copy-start(f32[120,256]{1,0:T(8,128)} %refs_0_.3) | copy-start | bytes 368644
  2.3 24.3 %copy-start.1 = (f32[120,256]{1,0:T(8,128)S(1)}, f32[120,256]{1,0:T(8,128)}, u32[]{:S(2)}) copy-start(f32[120,256]{1,0:T(8,128)} %refs_1_.3) | copy-start | bytes 368644
  2.3 24.3 %copy-start.2 = (f32[120,256]{1,0:T(8,128)S(1)}, f32[120,256]{1,0:T(8,128)}, u32[]{:S(2)}) copy-start(f32[120,256]{1,0:T(8,128)} %refs_2_.3) | copy-start | bytes 368644
  2.3 24.3 %copy-start.3 = (f32[120,256]{1,0:T(8,128)S(1)}, f32[120,256]{1,0:T(8,128)}, u32[]{:S(2)}) copy-start(f32[120,256]{1,0:T(8,128)} %refs_3_.3) | copy-start | bytes 368644
  2.3 24.3 %copy-start.4 = (s32[120,256]{1,0:T(8,128)S(1)}, s32[120,256]{1,0:T(8,128)}, u32[]{:S(2)}) copy-start(s32[120,256]{1,0:T(8,128)} %refs_4_.3) | copy-start | bytes 368644
  2.3 39.0 %all-to-all-start = ((f32[96,6,128]{2,1,0:T(8,128)}), f32[96,6,128]{2,1,0:T(8,128)S(1)}, u32[]{:S(2)}, u32[]{:S(2)}) async-start(f32[96,6,128]{2,1,0:T(8,128)} %raw.1), calls=%async_computation | async-start | bytes 786432 | tf_op jit(solution)/shard_map/all_to_all | solution.py:452
  26.5 0.7 %copy-start.5 = (s32[120]{0:T(128)S(1)}, s32[120]{0:T(128)}, u32[]{:S(2)}) copy-start(s32[120]{0:T(128)} %param.17) | copy-start | bytes 1444
  27.2 3.6 %copy-start.6 = (s32[3072]{0:T(1024)S(1)}, s32[3072]{0:T(1024)}, u32[]{:S(2)}) copy-start(s32[3072]{0:T(1024)} %param.21) | copy-start | bytes 36868
  27.2 3.6 %copy-start.7 = (s32[3072]{0:T(1024)S(1)}, s32[3072]{0:T(1024)}, u32[]{:S(2)}) copy-start(s32[3072]{0:T(1024)} %param.20) | copy-start | bytes 36868
  27.2 3.6 %copy-start.8 = (s32[3072]{0:T(1024)S(1)}, s32[3072]{0:T(1024)}, u32[]{:S(2)}) copy-start(s32[3072]{0:T(1024)} %param.19) | copy-start | bytes 36868
  27.3 4.3 %collective-permute-start = (f32[48,256]{1,0:T(8,128)S(1)}, f32[48,256]{1,0:T(8,128)S(1)}, u32[]{:S(2)}, u32[]{:S(2)}) collective-permute-start(f32[48,256]{1,0:T(8,128)S(1)} %get-tuple-element.5), channel_id=1, source_target_pairs={{0,8},{8,16},{16,24},{24,32},{32,40},{40,48},{48,56},{56,64},{64,7... | collective-permute-start | bytes 147464 | tf_op jit(solution)/shard_map/ppermute | solution.py:462
  29.5 6.4 %collective-permute-start.1 = (f32[48,256]{1,0:T(8,128)S(1)}, f32[48,256]{1,0:T(8,128)S(1)}, u32[]{:S(2)}, u32[]{:S(2)}) collective-permute-start(f32[48,256]{1,0:T(8,128)S(1)} %get-tuple-element.6), channel_id=1, source_target_pairs={{8,0},{16,8},{24,16},{32,24},{40,32},{48,40},{56,48},{64,56},{72,6... | collective-permute-start | bytes 147464 | tf_op jit(solution)/shard_map/ppermute | solution.py:462

commit v5 on v4

--- a/solution.py
+++ b/solution.py
@@ -39,7 +39,7 @@
 FIRST_COL = 5
 ROW_GROUP = [[(n + FIRST_ROW) % N_GY for n in range(N_GY)]]
 COL_GROUP = [[(n + FIRST_COL) % N_GX for n in range(N_GX)]]
-PARTS = 3
+PARTS = 2
 
 
 def iota(shape, dim):
@@ -243,10 +243,12 @@
     )
 
 
-def half_step(e, u, v, rub, push, inside):
+def half_step(e, u, v, rub, push, inside, emit=None):
     spread = pltpu.roll(u, WIDE - 1, 1) - pltpu.roll(u, 1, 1)
     spread = spread + (pltpu.roll(v, EXT - 1, 0) - pltpu.roll(v, 1, 0))
     mid = jnp.where(inside, e - C_MASS * spread, 0.0)
+    if emit is not None:
+        emit(0, mid)
     scale = 1.0 / (1.0 + rub * jnp.sqrt(u * u + v * v))
     slope_x = pltpu.roll(mid, WIDE - 1, 1) - pltpu.roll(mid, 1, 1)
     slope_y = pltpu.roll(mid, EXT - 1, 0) - pltpu.roll(mid, 1, 0)
@@ -308,7 +310,13 @@
 
 
 def step_kernel(smap, code, loads, cells, *refs):
-    *fields, up, down, out_eta, out_u, out_v, force, fringe = refs
+    *fields, up, down, out_eta, out_u, out_v, force, fringe, staged, sems = refs
+    outs = (out_eta, out_u, out_v)
+
+    def send(n, field):
+        staged[n] = field[HALO : HALO + ROWS, :COLS]
+        pltpu.make_async_copy(staged.at[n], outs[n], sems.at[n]).start()
+
     gy = lax.axis_index("gy")
     gx = lax.axis_index("gx")
     for start in range(0, PLAT, CHUNK):
@@ -383,21 +391,27 @@
             ],
             axis=1,
         )
-        return jnp.where(inside, u, 0.0), jnp.where(inside, v, 0.0)
+        u = jnp.where(inside, u, 0.0)
+        if step == SUBSTEPS - 1:
+            send(1, u)
+        return u, jnp.where(inside, v, 0.0)
 
     e = mid
     u, v = finish(0, e, flow_u - force_x * scale, flow_v - force_y * scale)
     for step in range(1, SUBSTEPS):
-        e, u, v, s = half_step(e, u, v, rub, push, inside)
+        emit = send if step == SUBSTEPS - 1 else None
+        e, u, v, s = half_step(e, u, v, rub, push, inside, emit)
         u, v = finish(step, e, u - force_x * s, v - force_y * s)
-    out_eta[...] = e[HALO : HALO + ROWS, :COLS]
-    out_u[...] = u[HALO : HALO + ROWS, :COLS]
-    out_v[...] = v[HALO : HALO + ROWS, :COLS]
-
-
-def call(kernel, out_shape, spaces, name, scratch=(), limit=12, cycles=1, **kw):
+    send(2, v)
+    for n in range(3):
+        pltpu.make_async_copy(staged.at[n], outs[n], sems.at[n]).wait()
+
+
+def call(
+    kernel, out_shape, spaces, name, scratch=(), limit=12, cycles=1, out_space=pltpu.VMEM, **kw
+):
     many = isinstance(out_shape, list)
-    out_spec = pl.BlockSpec(memory_space=pltpu.VMEM)
+    out_spec = pl.BlockSpec(memory_space=out_space)
     return pl.pallas_call(
         kernel,
         out_shape=out_shape,
@@ -485,9 +499,11 @@
     force = [
         pltpu.VMEM((2 * PARTS * EXT, COLS), jnp.float32),
         pltpu.VMEM((EXT, 128), jnp.float32),
+        pltpu.VMEM((3, ROWS, COLS), jnp.float32),
+        sems((3,)),
     ]
     return tuple(
-        call(step_kernel, [out, out, out], [vmem] * 11, "steps", force)(
+        call(step_kernel, [out, out, out], [vmem] * 11, "steps", force, out_space=hbm)(
             smap, code, loads, cells, *near
         )
     )

time: 64.8 us -> 64.4 us (level)
  no operation moved by 1% of the time
where the time goes in v5:
time: 64.4 us; the launch traced here: 64 us
  starting transfers between devices  27.8 us (43%)
  blocking collectives  17.9 us (28%)
  Pallas kernels  8.48 us (13%)
  waiting for transfers between devices  7.73 us (12%)
  local copies, waits for them, and re-layouts  1.33 us (2%)
  between operations  0.83 us (1%)
    all_to_all x1, starting transfers between devices, on_device(): lax.all_to_all(held, 'gy', 0, 0, axis_index_groups=ROW_GROUP, tiled=True)  24.2 us
    all_to_all x2, blocking collectives, on_device(): lax.all_to_all(slots, 'gx', 0, 0, axis_index_groups=COL_GROUP, tiled=True)  17.9 us
    ppermute x1, waiting for transfers between devices, on_device(): lax.ppermute(top, 'gy', downward)  4.28 us
    pallas_call x1, Pallas kernels, on_device(): call(step_kernel, [out, out, out], [vmem] * 11, 'steps', force, out_space...  3.95 us
    all_to_all x1, waiting for transfers between devices, on_device(): lax.all_to_all(held, 'gy', 0, 0, axis_index_groups=ROW_GROUP, tiled=True)  3.45 us
    ppermute x1, starting transfers between devices, on_device(): lax.ppermute(bottom, 'gy', upward)  2.23 us
    pallas_call x1, Pallas kernels, on_device(): call(cell_kernel, f32(N_GX, SLOT_ROWS, 128), [vmem] * 8, 'cells', cycles=4)  2.02 us
    pallas_call x1, Pallas kernels, on_device(): call(raw_kernel, f32(N_GY, 6, 128), [hbm] * 3, 'raw', [pltpu.VMEM((HELD,...  1.6 us
  transfers between devices with their start and end apart: 3, of which 2 were waited for; matrix products, arithmetic and copies ran while one was open for 1% of the time, Pallas kernels for 3%

profile of v5, /device:TPU:1, one launch (start us, length us, event | category | flops | bytes accessed | tf_op | source)
XLA Modules:
  0.0 64.0 jit_solution(12302959518348190281)
XLA Ops:
  0.6 1.6 %raw.1 = f32[96,6,128]{2,1,0:T(8,128)} custom-call(f32[4,60]{1,0:T(4,128)} %bitcast.12, f32[2,4,60]{2,1,0:T(4,128)} %bitcast.11, f32[2,3,2,4]{3,2,1,0:T(2,128)} %bitcast.10), custom_call_target="tpu_custom_call" | custom-call | flops 100000000 | bytes 2000000 | tf_op jit(solution)/shard_map/raw/pallas_call | solution.py:453
  2.2 0.0 copy-start
  2.3 0.0 copy-start.1
  2.3 0.0 copy-start.2
  2.3 0.0 copy-start.3
  2.3 0.0 copy-start.4
  2.3 24.2 %all-to-all-start = ((f32[96,6,128]{2,1,0:T(8,128)}), f32[96,6,128]{2,1,0:T(8,128)S(1)}, u32[]{:S(2)}, u32[]{:S(2)}) async-start(f32[96,6,128]{2,1,0:T(8,128)} %raw.1), calls=%async_computation | async-start | bytes 786432 | tf_op jit(solution)/shard_map/all_to_all | solution.py:466
  26.5 0.0 copy-start.5
  26.6 0.0 copy-done
  26.6 0.0 copy-done.1
  26.6 0.0 copy-done.2
  26.6 0.0 copy-done.3
  26.6 0.0 copy-done.4
  26.6 0.6 copy-done.5
  27.2 0.0 copy-start.6
  27.2 0.0 copy-start.7
  27.2 0.0 copy-start.8
  27.2 0.1 row_halo.1
  27.3 2.2 %collective-permute-start = (f32[48,256]{1,0:T(8,128)S(1)}, f32[48,256]{1,0:T(8,128)S(1)}, u32[]{:S(2)}, u32[]{:S(2)}) collective-permute-start(f32[48,256]{1,0:T(8,128)S(1)} %get-tuple-element.5), channel_id=1, source_target_pairs={{0,8},{8,16},{16,24},{24,32},{32,40},{40,48},{48,56},{56,64},{64,7... | collective-permute-start | bytes 147464 | tf_op jit(solution)/shard_map/ppermute | solution.py:476
  29.5 1.3 %collective-permute-start.1 = (f32[48,256]{1,0:T(8,128)S(1)}, f32[48,256]{1,0:T(8,128)S(1)}, u32[]{:S(2)}, u32[]{:S(2)}) collective-permute-start(f32[48,256]{1,0:T(8,128)S(1)} %get-tuple-element.6), channel_id=1, source_target_pairs={{8,0},{16,8},{24,16},{32,24},{40,32},{48,40},{56,48},{64,56},{72,6... | collective-permute-start | bytes 147464 | tf_op jit(solution)/shard_map/ppermute | solution.py:476
  30.8 0.0 copy-done.6
  30.8 0.0 copy-done.7
  30.8 0.0 copy-done.8
  30.9 0.4 reshape.16
  31.3 0.2 copy.16
  31.5 0.1 reshape.17.code
  31.6 0.0 collective-permute-done.refs_5_
  31.6 4.3 %collective-permute-done.1.refs_6_ = f32[48,256]{1,0:T(8,128)S(1)} collective-permute-done((f32[48,256]{1,0:T(8,128)S(1)}, f32[48,256]{1,0:T(8,128)S(1)}, u32[]{:S(2)}, u32[]{:S(2)}) %collective-permute-start.1) | collective-permute-done | bytes 49184 | tf_op jit(solution)/shard_map/ppermute | solution.py:476
  35.9 2.0 %cells.1.slots_in = f32[8,64,128]{2,1,0:T(8,128)S(1)} custom-call(s32[1,3072]{1,0:T(1,128)S(1)} %reshape.17.code, f32[120,256]{1,0:T(8,128)S(1)} %copy-done, f32[120,256]{1,0:T(8,128)S(1)} %copy-done.1, f32[120,256]{1,0:T(8,128)S(1)} %copy-done.2, f32[120,256]{1,0:T(8,128)S(1)} %copy-done.3, s32[120,256]{1,0:T(8,128)S(1)} %copy-done.4, ...), custom_call_target="tpu_custom_call" | custom-call | flops 400000000 | bytes 8000000 | tf_op jit(solution)/shard_map/cells/pallas_call | solution.py:481
  37.9 3.4 %all-to-all-done.raw = f32[96,6,128]{2,1,0:T(8,128)S(1)} async-done(((f32[96,6,128]{2,1,0:T(8,128)}), f32[96,6,128]{2,1,0:T(8,128)S(1)}, u32[]{:S(2)}, u32[]{:S(2)}) %all-to-all-start) | async-done | bytes 294944 | tf_op jit(solution)/shard_map/all_to_all | solution.py:466
  41.3 0.1 strips.1
  41.4 10.0 %all_to_all.15.cells = f32[8,64,128]{2,1,0:T(8,128)S(1)} all-to-all(f32[8,64,128]{2,1,0:T(8,128)S(1)} %strips.1), channel_id=1, replica_groups={{5,6,7,0,1,2,3,4},{13,14,15,8,9,10,11,12},{21,22,23,16,17,18,19,20},{29..., dimensions={0} | all-to-all | bytes 524288 | tf_op jit(solution)/shard_map/all_to_all | solution.py:495
  51.4 0.8 %loads.1 = f32[8,8,128]{2,1,0:T(8,128)S(1)} custom-call(f32[8,64,128]{2,1,0:T(8,128)S(1)} %all_to_all.15.cells, f32[96,6,128]{2,1,0:T(8,128)S(1)} %all-to-all-done.raw), custom_call_target="tpu_custom_call" | custom-call | flops 100000000 | bytes 2000000 | tf_op jit(solution)/shard_map/loads/pallas_call | solution.py:496
  52.2 7.9 %all_to_all.16.loads = f32[8,8,128]{2,1,0:T(8,128)S(1)} all-to-all(f32[8,8,128]{2,1,0:T(8,128)S(1)} %loads.1), channel_id=1, replica_groups={{5,6,7,0,1,2,3,4},{13,14,15,8,9,10,11,12},{21,22,23,16,17,18,19,20},{29..., dimensions={0} | all-to-all | bytes 65536 | tf_op jit(solution)/shard_map/all_to_all | solution.py:497
  60.0 4.0 %steps.1 = (f32[120,256]{1,0:T(8,128)}, f32[120,256]{1,0:T(8,128)}, f32[120,256]{1,0:T(8,128)}) custom-call(s32[1,120]{1,0:T(1,128)S(1)} %bitcast.7, s32[1,3072]{1,0:T(1,128)S(1)} %reshape.17.code, f32[8,8,128]{2,1,0:T(8,128)S(1)} %all_to_all.16.loads, f32[8,64,128]{2,1,0:T(8,128)S(1)} %all_to_all.15.cells, f32[120,256]{1,0:T(8,128)S(1)} %copy-done, ...), custom_call_target="tpu_custom_call" | custom-call | flops 100000000 | bytes 2000000 | tf_op jit(solution)/shard_map/steps/pallas_call | solution.py:506
  (3 shorter events, 0.0 us)
Async XLA Ops:
  2.2 24.3 %copy-start = (f32[120,256]{1,0:T(8,128)S(1)}, f32[120,256]{1,0:T(8,128)}, u32[]{:S(2)}) copy-start(f32[120,256]{1,0:T(8,128)} %refs_0_.3) | copy-start | bytes 368644
  2.3 24.3 %copy-start.1 = (f32[120,256]{1,0:T(8,128)S(1)}, f32[120,256]{1,0:T(8,128)}, u32[]{:S(2)}) copy-start(f32[120,256]{1,0:T(8,128)} %refs_1_.3) | copy-start | bytes 368644
  2.3 24.3 %copy-start.2 = (f32[120,256]{1,0:T(8,128)S(1)}, f32[120,256]{1,0:T(8,128)}, u32[]{:S(2)}) copy-start(f32[120,256]{1,0:T(8,128)} %refs_2_.3) | copy-start | bytes 368644
  2.3 24.3 %copy-start.3 = (f32[120,256]{1,0:T(8,128)S(1)}, f32[120,256]{1,0:T(8,128)}, u32[]{:S(2)}) copy-start(f32[120,256]{1,0:T(8,128)} %refs_3_.3) | copy-start | bytes 368644
  2.3 24.3 %copy-start.4 = (s32[120,256]{1,0:T(8,128)S(1)}, s32[120,256]{1,0:T(8,128)}, u32[]{:S(2)}) copy-start(s32[120,256]{1,0:T(8,128)} %refs_4_.3) | copy-start | bytes 368644
  2.3 39.0 %all-to-all-start = ((f32[96,6,128]{2,1,0:T(8,128)}), f32[96,6,128]{2,1,0:T(8,128)S(1)}, u32[]{:S(2)}, u32[]{:S(2)}) async-start(f32[96,6,128]{2,1,0:T(8,128)} %raw.1), calls=%async_computation | async-start | bytes 786432 | tf_op jit(solution)/shard_map/all_to_all | solution.py:466
  26.5 0.7 %copy-start.5 = (s32[120]{0:T(128)S(1)}, s32[120]{0:T(128)}, u32[]{:S(2)}) copy-start(s32[120]{0:T(128)} %param.17) | copy-start | bytes 1444
  27.2 3.6 %copy-start.6 = (s32[3072]{0:T(1024)S(1)}, s32[3072]{0:T(1024)}, u32[]{:S(2)}) copy-start(s32[3072]{0:T(1024)} %param.21) | copy-start | bytes 36868
  27.2 3.6 %copy-start.7 = (s32[3072]{0:T(1024)S(1)}, s32[3072]{0:T(1024)}, u32[]{:S(2)}) copy-start(s32[3072]{0:T(1024)} %param.20) | copy-start | bytes 36868
  27.2 3.6 %copy-start.8 = (s32[3072]{0:T(1024)S(1)}, s32[3072]{0:T(1024)}, u32[]{:S(2)}) copy-start(s32[3072]{0:T(1024)} %param.19) | copy-start | bytes 36868
  27.3 4.3 %collective-permute-start = (f32[48,256]{1,0:T(8,128)S(1)}, f32[48,256]{1,0:T(8,128)S(1)}, u32[]{:S(2)}, u32[]{:S(2)}) collective-permute-start(f32[48,256]{1,0:T(8,128)S(1)} %get-tuple-element.5), channel_id=1, source_target_pairs={{0,8},{8,16},{16,24},{24,32},{32,40},{40,48},{48,56},{56,64},{64,7... | collective-permute-start | bytes 147464 | tf_op jit(solution)/shard_map/ppermute | solution.py:476
  29.5 6.4 %collective-permute-start.1 = (f32[48,256]{1,0:T(8,128)S(1)}, f32[48,256]{1,0:T(8,128)S(1)}, u32[]{:S(2)}, u32[]{:S(2)}) collective-permute-start(f32[48,256]{1,0:T(8,128)S(1)} %get-tuple-element.6), channel_id=1, source_target_pairs={{8,0},{16,8},{24,16},{32,24},{40,32},{48,40},{56,48},{64,56},{72,6... | collective-permute-start | bytes 147464 | tf_op jit(solution)/shard_map/ppermute | solution.py:476

commit v6 on v5

--- a/solution.py
+++ b/solution.py
@@ -32,13 +32,15 @@
 SPAN = FIELDS * HALO
 CELL_ROW = GROUP
 STRIP_ROW = GROUP + 9
-SLOT_ROWS = 64
+SLOT_ROWS = 62
 BACK_ROWS = 8
 CHUNK = 512
 FIRST_ROW = 68
 FIRST_COL = 5
 ROW_GROUP = [[(n + FIRST_ROW) % N_GY for n in range(N_GY)]]
 COL_GROUP = [[(n + FIRST_COL) % N_GX for n in range(N_GX)]]
+FIRST_BACK = 3
+BACK_GROUP = [[(n + FIRST_BACK) % N_GX for n in range(N_GX)]]
 PARTS = 2
 
 
@@ -333,7 +335,7 @@
         for c in range(2):
             line = jnp.concatenate(
                 [
-                    loads[col_slot(b // 3), 3 * c + b % 3 : 3 * c + b % 3 + 1, :]
+                    loads[(b // 3 - FIRST_BACK) % N_GX, 3 * c + b % 3 : 3 * c + b % 3 + 1, :]
                     for b in range(start // 128, (start + CHUNK) // 128)
                 ],
                 axis=1,
@@ -494,7 +496,7 @@
     )(raw, slots)
     cells = lax.all_to_all(slots, "gx", 0, 0, axis_index_groups=COL_GROUP, tiled=True)
     slots = call(load_kernel, f32(N_GX, BACK_ROWS, 128), [vmem, vmem], "loads")(cells, raw)
-    loads = lax.all_to_all(slots, "gx", 0, 0, axis_index_groups=COL_GROUP, tiled=True)
+    loads = lax.all_to_all(slots, "gx", 0, 0, axis_index_groups=BACK_GROUP, tiled=True)
     out = f32(ROWS, COLS)
     force = [
         pltpu.VMEM((2 * PARTS * EXT, COLS), jnp.float32),

time: 64.4 us -> 65.6 us (1.019)
  blocking collectives: 17.9 us -> 19.1 us
    all_to_all x0 -> x1, blocking collectives: none -> 9.1 us  [on_device(): lax.all_to_all(slots, 'gx', 0, 0, axis_index_groups=BACK_GROUP, tiled=True)]
    all_to_all x2 -> x1, blocking collectives: 17.9 us -> 9.97 us  [on_device(): lax.all_to_all(slots, 'gx', 0, 0, axis_index_groups=COL_GROUP, tiled=True)]
where the time goes in v6:
time: 65.6 us; the launch traced here: 65.2 us
  starting transfers between devices  27.8 us (42%)
  blocking collectives  19.1 us (29%)
  Pallas kernels  8.48 us (13%)
  waiting for transfers between devices  7.73 us (12%)
  local copies, waits for them, and re-layouts  1.33 us (2%)
  between operations  0.83 us (1%)
    all_to_all x1, starting transfers between devices, on_device(): lax.all_to_all(held, 'gy', 0, 0, axis_index_groups=ROW_GROUP, tiled=True)  24.2 us
    all_to_all x1, blocking collectives, on_device(): lax.all_to_all(slots, 'gx', 0, 0, axis_index_groups=COL_GROUP, tiled=True)  9.97 us
    all_to_all x1, blocking collectives, on_device(): lax.all_to_all(slots, 'gx', 0, 0, axis_index_groups=BACK_GROUP, tiled=True)  9.1 us
    ppermute x1, waiting for transfers between devices, on_device(): lax.ppermute(top, 'gy', downward)  4.28 us
    pallas_call x1, Pallas kernels, on_device(): call(step_kernel, [out, out, out], [vmem] * 11, 'steps', force, out_space...  3.96 us
    all_to_all x1, waiting for transfers between devices, on_device(): lax.all_to_all(held, 'gy', 0, 0, axis_index_groups=ROW_GROUP, tiled=True)  3.45 us
    ppermute x1, starting transfers between devices, on_device(): lax.ppermute(bottom, 'gy', upward)  2.23 us
    pallas_call x1, Pallas kernels, on_device(): call(cell_kernel, f32(N_GX, SLOT_ROWS, 128), [vmem] * 8, 'cells', cycles=4)  2.02 us
  transfers between devices with their start and end apart: 3, of which 2 were waited for; matrix products, arithmetic and copies ran while one was open for 1% of the time, Pallas kernels for 3%

profile of v6, /device:TPU:1, one launch (start us, length us, event | category | flops | bytes accessed | tf_op | source)
XLA Modules:
  0.0 65.2 jit_solution(14640063174590097442)
XLA Ops:
  0.6 1.6 %raw.1 = f32[96,6,128]{2,1,0:T(8,128)} custom-call(f32[4,60]{1,0:T(4,128)} %bitcast.12, f32[2,4,60]{2,1,0:T(4,128)} %bitcast.11, f32[2,3,2,4]{3,2,1,0:T(2,128)} %bitcast.10), custom_call_target="tpu_custom_call" | custom-call | flops 100000000 | bytes 2000000 | tf_op jit(solution)/shard_map/raw/pallas_call | solution.py:455
  2.2 0.0 copy-start
  2.3 0.0 copy-start.1
  2.3 0.0 copy-start.2
  2.3 0.0 copy-start.3
  2.3 0.0 copy-start.4
  2.3 24.2 %all-to-all-start = ((f32[96,6,128]{2,1,0:T(8,128)}), f32[96,6,128]{2,1,0:T(8,128)S(1)}, u32[]{:S(2)}, u32[]{:S(2)}) async-start(f32[96,6,128]{2,1,0:T(8,128)} %raw.1), calls=%async_computation | async-start | bytes 786432 | tf_op jit(solution)/shard_map/all_to_all | solution.py:468
  26.5 0.0 copy-start.5
  26.6 0.0 copy-done
  26.6 0.0 copy-done.1
  26.6 0.0 copy-done.2
  26.6 0.0 copy-done.3
  26.6 0.0 copy-done.4
  26.6 0.6 copy-done.5
  27.2 0.0 copy-start.6
  27.2 0.0 copy-start.7
  27.2 0.0 copy-start.8
  27.2 0.1 row_halo.1
  27.3 2.2 %collective-permute-start = (f32[48,256]{1,0:T(8,128)S(1)}, f32[48,256]{1,0:T(8,128)S(1)}, u32[]{:S(2)}, u32[]{:S(2)}) collective-permute-start(f32[48,256]{1,0:T(8,128)S(1)} %get-tuple-element.5), channel_id=1, source_target_pairs={{0,8},{8,16},{16,24},{24,32},{32,40},{40,48},{48,56},{56,64},{64,7... | collective-permute-start | bytes 147464 | tf_op jit(solution)/shard_map/ppermute | solution.py:478
  29.5 1.3 %collective-permute-start.1 = (f32[48,256]{1,0:T(8,128)S(1)}, f32[48,256]{1,0:T(8,128)S(1)}, u32[]{:S(2)}, u32[]{:S(2)}) collective-permute-start(f32[48,256]{1,0:T(8,128)S(1)} %get-tuple-element.6), channel_id=1, source_target_pairs={{8,0},{16,8},{24,16},{32,24},{40,32},{48,40},{56,48},{64,56},{72,6... | collective-permute-start | bytes 147464 | tf_op jit(solution)/shard_map/ppermute | solution.py:478
  30.8 0.0 copy-done.6
  30.8 0.0 copy-done.7
  30.8 0.0 copy-done.8
  30.9 0.4 reshape.16
  31.3 0.2 copy.16
  31.5 0.1 reshape.17.code
  31.6 0.0 collective-permute-done.refs_5_
  31.6 4.3 %collective-permute-done.1.refs_6_ = f32[48,256]{1,0:T(8,128)S(1)} collective-permute-done((f32[48,256]{1,0:T(8,128)S(1)}, f32[48,256]{1,0:T(8,128)S(1)}, u32[]{:S(2)}, u32[]{:S(2)}) %collective-permute-start.1) | collective-permute-done | bytes 49184 | tf_op jit(solution)/shard_map/ppermute | solution.py:478
  35.9 2.0 %cells.1.slots_in = f32[8,62,128]{2,1,0:T(8,128)S(1)} custom-call(s32[1,3072]{1,0:T(1,128)S(1)} %reshape.17.code, f32[120,256]{1,0:T(8,128)S(1)} %copy-done, f32[120,256]{1,0:T(8,128)S(1)} %copy-done.1, f32[120,256]{1,0:T(8,128)S(1)} %copy-done.2, f32[120,256]{1,0:T(8,128)S(1)} %copy-done.3, s32[120,256]{1,0:T(8,128)S(1)} %copy-done.4, ...), custom_call_target="tpu_custom_call" | custom-call | flops 400000000 | bytes 8000000 | tf_op jit(solution)/shard_map/cells/pallas_call | solution.py:483
  37.9 3.4 %all-to-all-done.raw = f32[96,6,128]{2,1,0:T(8,128)S(1)} async-done(((f32[96,6,128]{2,1,0:T(8,128)}), f32[96,6,128]{2,1,0:T(8,128)S(1)}, u32[]{:S(2)}, u32[]{:S(2)}) %all-to-all-start) | async-done | bytes 294944 | tf_op jit(solution)/shard_map/all_to_all | solution.py:468
  41.3 0.1 strips.1
  41.4 10.0 %all_to_all.15.cells = f32[8,62,128]{2,1,0:T(8,128)S(1)} all-to-all(f32[8,62,128]{2,1,0:T(8,128)S(1)} %strips.1), channel_id=1, replica_groups={{5,6,7,0,1,2,3,4},{13,14,15,8,9,10,11,12},{21,22,23,16,17,18,19,20},{29..., dimensions={0} | all-to-all | bytes 507904 | tf_op jit(solution)/shard_map/all_to_all | solution.py:497
  51.4 0.8 %loads.1 = f32[8,8,128]{2,1,0:T(8,128)S(1)} custom-call(f32[8,62,128]{2,1,0:T(8,128)S(1)} %all_to_all.15.cells, f32[96,6,128]{2,1,0:T(8,128)S(1)} %all-to-all-done.raw), custom_call_target="tpu_custom_call" | custom-call | flops 100000000 | bytes 2000000 | tf_op jit(solution)/shard_map/loads/pallas_call | solution.py:498
  52.2 9.1 %all_to_all.16.loads = f32[8,8,128]{2,1,0:T(8,128)S(1)} all-to-all(f32[8,8,128]{2,1,0:T(8,128)S(1)} %loads.1), channel_id=1, replica_groups={{3,4,5,6,7,0,1,2},{11,12,13,14,15,8,9,10},{19,20,21,22,23,16,17,18},{27..., dimensions={0} | all-to-all | bytes 65536 | tf_op jit(solution)/shard_map/all_to_all | solution.py:499
  61.3 4.0 %steps.1 = (f32[120,256]{1,0:T(8,128)}, f32[120,256]{1,0:T(8,128)}, f32[120,256]{1,0:T(8,128)}) custom-call(s32[1,120]{1,0:T(1,128)S(1)} %bitcast.7, s32[1,3072]{1,0:T(1,128)S(1)} %reshape.17.code, f32[8,8,128]{2,1,0:T(8,128)S(1)} %all_to_all.16.loads, f32[8,62,128]{2,1,0:T(8,128)S(1)} %all_to_all.15.cells, f32[120,256]{1,0:T(8,128)S(1)} %copy-done, ...), custom_call_target="tpu_custom_call" | custom-call | flops 100000000 | bytes 2000000 | tf_op jit(solution)/shard_map/steps/pallas_call | solution.py:508
  (3 shorter events, 0.0 us)
Async XLA Ops:
  2.2 24.3 %copy-start = (f32[120,256]{1,0:T(8,128)S(1)}, f32[120,256]{1,0:T(8,128)}, u32[]{:S(2)}) copy-start(f32[120,256]{1,0:T(8,128)} %refs_0_.3) | copy-start | bytes 368644
  2.3 24.3 %copy-start.1 = (f32[120,256]{1,0:T(8,128)S(1)}, f32[120,256]{1,0:T(8,128)}, u32[]{:S(2)}) copy-start(f32[120,256]{1,0:T(8,128)} %refs_1_.3) | copy-start | bytes 368644
  2.3 24.3 %copy-start.2 = (f32[120,256]{1,0:T(8,128)S(1)}, f32[120,256]{1,0:T(8,128)}, u32[]{:S(2)}) copy-start(f32[120,256]{1,0:T(8,128)} %refs_2_.3) | copy-start | bytes 368644
  2.3 24.3 %copy-start.3 = (f32[120,256]{1,0:T(8,128)S(1)}, f32[120,256]{1,0:T(8,128)}, u32[]{:S(2)}) copy-start(f32[120,256]{1,0:T(8,128)} %refs_3_.3) | copy-start | bytes 368644
  2.3 24.3 %copy-start.4 = (s32[120,256]{1,0:T(8,128)S(1)}, s32[120,256]{1,0:T(8,128)}, u32[]{:S(2)}) copy-start(s32[120,256]{1,0:T(8,128)} %refs_4_.3) | copy-start | bytes 368644
  2.3 39.0 %all-to-all-start = ((f32[96,6,128]{2,1,0:T(8,128)}), f32[96,6,128]{2,1,0:T(8,128)S(1)}, u32[]{:S(2)}, u32[]{:S(2)}) async-start(f32[96,6,128]{2,1,0:T(8,128)} %raw.1), calls=%async_computation | async-start | bytes 786432 | tf_op jit(solution)/shard_map/all_to_all | solution.py:468
  26.5 0.7 %copy-start.5 = (s32[120]{0:T(128)S(1)}, s32[120]{0:T(128)}, u32[]{:S(2)}) copy-start(s32[120]{0:T(128)} %param.17) | copy-start | bytes 1444
  27.2 3.6 %copy-start.6 = (s32[3072]{0:T(1024)S(1)}, s32[3072]{0:T(1024)}, u32[]{:S(2)}) copy-start(s32[3072]{0:T(1024)} %param.21) | copy-start | bytes 36868
  27.2 3.6 %copy-start.7 = (s32[3072]{0:T(1024)S(1)}, s32[3072]{0:T(1024)}, u32[]{:S(2)}) copy-start(s32[3072]{0:T(1024)} %param.20) | copy-start | bytes 36868
  27.2 3.6 %copy-start.8 = (s32[3072]{0:T(1024)S(1)}, s32[3072]{0:T(1024)}, u32[]{:S(2)}) copy-start(s32[3072]{0:T(1024)} %param.19) | copy-start | bytes 36868
  27.3 4.3 %collective-permute-start = (f32[48,256]{1,0:T(8,128)S(1)}, f32[48,256]{1,0:T(8,128)S(1)}, u32[]{:S(2)}, u32[]{:S(2)}) collective-permute-start(f32[48,256]{1,0:T(8,128)S(1)} %get-tuple-element.5), channel_id=1, source_target_pairs={{0,8},{8,16},{16,24},{24,32},{32,40},{40,48},{48,56},{56,64},{64,7... | collective-permute-start | bytes 147464 | tf_op jit(solution)/shard_map/ppermute | solution.py:478
  29.5 6.4 %collective-permute-start.1 = (f32[48,256]{1,0:T(8,128)S(1)}, f32[48,256]{1,0:T(8,128)S(1)}, u32[]{:S(2)}, u32[]{:S(2)}) collective-permute-start(f32[48,256]{1,0:T(8,128)S(1)} %get-tuple-element.6), channel_id=1, source_target_pairs={{8,0},{16,8},{24,16},{32,24},{40,32},{48,40},{56,48},{64,56},{72,6... | collective-permute-start | bytes 147464 | tf_op jit(solution)/shard_map/ppermute | solution.py:478
